TPU v7x, 256 devices: a whole 4x4x8 slice. The times are simulated.
256 devices in a mesh: row: 8 (over z_lo, x), col: 32 (over y, z_hi, core).
Axes of the slice: x: 4, y: 4, z: 8 (z_hi: 4, z_lo: 2; z = z_hi * 2 + z_lo), core: 2. Of those that a mesh axis runs over, the one named last changes fastest.
Arguments:
- tokens: bfloat16 [4096, 6144], P('row', 'col'), may hold values from -6 to 6
- weight: bfloat16 [6144, 24576], P('row', 'col'), may hold values from -0.078125 to 0.078125
- grad_out: bfloat16 [4096, 24576], P('row', 'col'), may hold values from -6 to 6
Outputs:
- activated: bfloat16 [4096, 24576], P('row', 'col')
- grad_tokens: bfloat16 [4096, 6144], P('row', 'col')
- grad_weight: bfloat16 [6144, 24576], P('row', 'col')
All inputs are finite; a program needn't handle non-finite values.
Results may differ from a plain program's by a relative error of at most 0.025.
Values may be sent and summed in bfloat16 or wider, within the bound.
No kernel may reach another device: no remote copies, remote signals or barrier semaphores. Data moves between devices by JAX's collectives and lax.ppermute only.
A program may use at most 128 MiB of HBM per device.

v0:
```python
import math

import jax
import jax.numpy as jnp
from jax import lax
from jax.sharding import PartitionSpec as P

slope_coef = math.sqrt(2.0 / math.pi)


def gelu_value(values):
    inside_arg = slope_coef * (values + 0.044715 * values * values * values)
    return 0.5 * values * (1.0 + jnp.tanh(inside_arg))


def gelu_slope(values):
    inside_arg = slope_coef * (values + 0.044715 * values * values * values)
    tangent = jnp.tanh(inside_arg)
    return 0.5 * (1.0 + tangent) + 0.5 * values * (1.0 - tangent * tangent) * slope_coef * (
        1.0 + 3.0 * 0.044715 * values * values
    )


def per_device(tokens, weight, grad_out):
    gathered = lax.all_gather(tokens, "col", axis=1, tiled=True)
    trailing = (((1,), (1,)), ((), ()))
    columns = gathered
    pre_act = jnp.dot(
        columns,
        lax.all_gather(weight, "row", axis=0, tiled=True),
        preferred_element_type=jnp.float32,
    )
    activated = gelu_value(pre_act).astype(jnp.bfloat16)
    grad_pre = (grad_out.astype(jnp.float32) * gelu_slope(pre_act)).astype(jnp.bfloat16)
    partial_input = lax.dot_general(
        grad_pre,
        lax.all_gather(weight, "row", axis=0, tiled=True),
        trailing,
        preferred_element_type=jnp.float32,
    )
    grad_tokens = lax.psum_scatter(
        partial_input.astype(jnp.bfloat16), "col", scatter_dimension=1, tiled=True
    )
    columns = gathered
    grad_weight = lax.psum_scatter(
        lax.dot_general(
            columns, grad_pre, (((0,), (0,)), ((), ())), preferred_element_type=jnp.float32
        ).astype(jnp.bfloat16),
        "row",
        scatter_dimension=0,
        tiled=True,
    )
    return (activated, grad_tokens, grad_weight)


def solution(mesh):
    in_specs = (P("row", "col"), P("row", "col"), P("row", "col"))
    out_specs = (P("row", "col"), P("row", "col"), P("row", "col"))
    return jax.shard_map(
        per_device, mesh=mesh, in_specs=in_specs, out_specs=out_specs, check_vma=False
    )
```

profile of v0, /device:TPU:38, one launch (start us, length us, event | category | flops | bytes accessed | tf_op | source)
XLA Modules:
  0.0 429.0 jit_solution(11128048307028663390)
XLA Ops:
  7.2 0.0 all-gather.3.cloned.1.call-start
  7.2 0.7 all-gather.3.cloned.1.call-update
  7.9 0.0 all-gather.5.cloned.1.call-start
  7.9 0.7 all-gather.5.cloned.1.call-update
  8.6 0.0 copy-start.1
  8.7 0.0 reduce-scatter.5.cloned.1.call-start
  8.7 70.7 %all-gather.3.cloned.1.call-done = bf16[512,6144]{0,1:T(8,128)(2,1)} async-done(((bf16[512,192]{0,1:T(8,128)(2,1)}), bf16[512,6144]{0,1:T(8,128)(2,1)}) %all-gather.3.cloned.1.call-update) | async-done | bytes 6291472 | tf_op jit(solution)/shard_map/all_gather | solution.py:25
  79.4 104.0 %all-gather.5.cloned.1.call-done = bf16[6144,768]{1,0:T(8,128)(2,1)} async-done(((bf16[768,768]{1,0:T(8,128)(2,1)}), bf16[6144,768]{1,0:T(8,128)(2,1)}) %all-gather.5.cloned.1.call-update) | async-done | bytes 9437200 | tf_op jit(solution)/shard_map/all_gather | solution.py:30
  183.4 0.0 copy-start
  183.4 11.0 %multiply_convert_fusion = (bf16[512,768]{1,0:T(8,128)(2,1)}, f32[512,768]{1,0:T(8,128)S(1)}) fusion(bf16[512,6144]{0,1:T(8,128)(2,1)} %all-gather.3.cloned.1.call-done, bf16[6144,768]{1,0:T(8,128)(2,1)} %all-gather.5.cloned.1.call-done), kind=kOutput, calls=%fused_computation.12 | convolution fusion | flops 4835377152 | bytes 18087936 | tf_op jit(solution)/shard_map/dot_general | solution.py:28
  194.4 0.0 copy-done.1
  194.4 0.0 copy-done
  194.4 9.4 %fusion = bf16[6144,768]{0,1:T(8,128)(2,1)} fusion(bf16[512,6144]{0,1:T(8,128)(2,1)S(1)} %copy-done, f32[512,768]{1,0:T(8,128)S(1)} %get-tuple-element.7, bf16[512,768]{1,0:T(8,128)(2,1)S(1)} %copy-done.1), kind=kOutput, calls=%fused_computation.1 | convolution fusion | flops 4844421120 | bytes 18087936 | tf_op jit(solution)/shard_map/dot_general | solution.py:46
  203.8 0.0 reduce-scatter.5.cloned.1.call-update
  203.9 0.0 reduce-scatter.3.cloned.1.call-start
  203.9 11.3 %convolution_convert_fusion.1 = bf16[512,6144]{0,1:T(8,128)(2,1)} fusion(bf16[6144,768]{1,0:T(8,128)(2,1)} %all-gather.5.cloned.1.call-done, f32[512,768]{1,0:T(8,128)S(1)} %get-tuple-element.7, bf16[512,768]{1,0:T(8,128)(2,1)S(1)} %copy-done.1), kind=kOutput, calls=%fused_computation.2 | convolution fusion | flops 4842848256 | bytes 18087936 | tf_op jit(solution)/shard_map/dot_general | solution.py:35
  215.3 0.0 reduce-scatter.3.cloned.1.call-update
  215.3 92.7 %reduce-scatter.5.cloned.1.call-done = bf16[768,768]{0,1:T(8,128)(2,1)} async-done(((bf16[6144,768]{0,1:T(8,128)(2,1)}), bf16[768,768]{0,1:T(8,128)(2,1)}) %reduce-scatter.5.cloned.1.call-update) | async-done | bytes 1179664 | tf_op jit(solution)/shard_map/reduce_scatter | solution.py:45
  308.0 2.4 copy.6
  310.3 112.1 %reduce-scatter.3.cloned.1.call-done = bf16[512,192]{0,1:T(8,128)(2,1)} async-done(((bf16[512,6144]{0,1:T(8,128)(2,1)}), bf16[512,192]{0,1:T(8,128)(2,1)}) %reduce-scatter.3.cloned.1.call-update) | async-done | bytes 196624 | tf_op jit(solution)/shard_map/reduce_scatter | solution.py:41
Async XLA Ops:
  7.2 72.3 %all-gather.3.cloned.1.call-start = ((), (), s32[]{:S(2)}) async-start(), calls=%async_computation.2 | async-start | bytes 6488064 | tf_op jit(solution)/shard_map/all_gather | solution.py:25
  7.9 175.5 %all-gather.5.cloned.1.call-start = ((), (), s32[]{:S(2)}) async-start(), calls=%async_computation.3 | async-start | bytes 10616832 | tf_op jit(solution)/shard_map/all_gather | solution.py:30
  8.6 185.8 %copy-start.1 = (bf16[512,768]{1,0:T(8,128)(2,1)S(1)}, bf16[512,768]{1,0:T(8,128)(2,1)}, u32[]{:S(2)}) copy-start(bf16[512,768]{1,0:T(8,128)(2,1)} %param.5) | copy-start | bytes 2359300
  8.7 299.3 %reduce-scatter.5.cloned.1.call-start = ((), (), s32[]{:S(2)}) async-start(), calls=%async_computation.5 | async-start | bytes 10616832 | tf_op jit(solution)/shard_map/reduce_scatter | solution.py:45
  183.4 11.0 %copy-start = (bf16[512,6144]{0,1:T(8,128)(2,1)S(1)}, bf16[512,6144]{0,1:T(8,128)(2,1)}, u32[]{:S(2)}) copy-start(bf16[512,6144]{0,1:T(8,128)(2,1)} %all-gather.3.cloned.1.call-done) | copy-start | bytes 18874372
  203.9 218.6 %reduce-scatter.3.cloned.1.call-start = ((), (), s32[]{:S(2)}) async-start(), calls=%async_computation.4 | async-start | bytes 6488064 | tf_op jit(solution)/shard_map/reduce_scatter | solution.py:41
Sparse Core Ops, SparseCore 0:
  10.5 68.8 all-gather.2
  81.2 102.1 all-gather.4
  204.0 103.9 reduce-scatter.4
  312.4 109.9 reduce-scatter.2
where the time goes:
time: 431 us; the launch traced here: 429 us
  waiting for transfers between devices  381 us (88%)
  matrix products  31.8 us (7%)
  between operations  13.8 us (3%)
    reduce_scatter x1, waiting for transfers between devices, per_device(): lax.psum_scatter(partial_input.astype(jnp.bfloat16), 'col', scatter_dimen...  112 us
    all_gather x1, waiting for transfers between devices, per_device(): lax.all_gather(weight, 'row', axis=0, tiled=True)  104 us
    reduce_scatter x1, waiting for transfers between devices, per_device(): lax.psum_scatter(lax.dot_general(columns, grad_pre, (((0,), (0,)), ((), (...  92.7 us
    all_gather x1, waiting for transfers between devices, per_device(): gathered = lax.all_gather(tokens, 'col', axis=1, tiled=True)  70.7 us
    dot_general x1, matrix products, per_device(): lax.dot_general(grad_pre, lax.all_gather(weight, 'row', axis=0, tiled=Tru...  11.3 us
    dot_general x1, matrix products, per_device(): jnp.dot(columns, lax.all_gather(weight, 'row', axis=0, tiled=True), prefe...  11 us
    dot_general x1, matrix products, per_device(): lax.dot_general(columns, grad_pre, (((0,), (0,)), ((), ())), preferred_el...  9.41 us
  transfers between devices with their start and end apart: 4, of which 4 were waited for; matrix products, arithmetic and copies ran while one was open for 3% of the time, Pallas kernels for 0%

commit v1 on v0

v1 whole, which is shorter than its diff:
```python
import functools
import math

import jax
import jax.numpy as jnp
from jax import lax
from jax.experimental import pallas as pl
from jax.experimental.pallas import tpu as pltpu
from jax.sharding import Mesh
from jax.sharding import PartitionSpec as P

slope_coef = math.sqrt(2.0 / math.pi)
AXES = ("zl", "x", "y", "zh", "c")
SIZES = {"zl": 2, "x": 4, "y": 4, "zh": 4, "c": 2}
BF16, F32 = jnp.bfloat16, jnp.float32
VMEM_LIMIT = 40 * 1024 * 1024
HBM = pl.BlockSpec(memory_space=pl.ANY)
VMEM = pl.BlockSpec(memory_space=pltpu.VMEM)
SMEM = pl.BlockSpec(memory_space=pltpu.SMEM)


def flip(value, axis, mask):
    return lax.ppermute(value, axis, [(i, i ^ mask) for i in range(SIZES[axis])])


def over_z(value):
    return flip(value, "zl", 1)


def spread_pairs():
    pairs = []
    for zl in range(2):
        for y in range(4):
            to_y = y if y >> 1 == zl else y ^ 3
            pairs.append((zl * 4 + y, (y >> 1) * 4 + to_y))
    return pairs


def spread(value):
    return lax.ppermute(value, ("zl", "y"), spread_pairs())


def spread_back(value):
    return lax.ppermute(value, ("zl", "y"), [(b, a) for a, b in spread_pairs()])


def call(kernel, out_shape, in_specs, out_specs, scratch, flops, nbytes):
    return pl.pallas_call(
        kernel,
        out_shape=out_shape,
        in_specs=in_specs,
        out_specs=out_specs,
        scratch_shapes=scratch,
        compiler_params=pltpu.CompilerParams(vmem_limit_bytes=VMEM_LIMIT),
        cost_estimate=pl.CostEstimate(flops=flops, bytes_accessed=nbytes, transcendentals=0),
    )


def run_copies(copies):
    for copy in copies:
        copy.start()
    for copy in copies:
        copy.wait()


def weight_row(idx, near, dz, dc):
    zl, y, zh, c = idx[0], idx[2], idx[3], idx[4]
    upper = near ^ zl ^ (y & 1) ^ (y >> 1)
    return pl.multiple_of(((upper * 4 + (zh ^ dz)) * 2 + (c ^ dc)) * 192, 192)


def arrange_kernel(idx, w, out, sems):
    copies = []
    for dc in range(2):
        for near in range(2):
            for dz in range(4):
                copies.append(
                    pltpu.make_async_copy(
                        w.at[pl.ds(weight_row(idx, near, dz, dc), 192), :],
                        out.at[dc, pl.ds((near * 4 + dz) * 192, 192), :],
                        sems.at[len(copies)],
                    )
                )
    run_copies(copies)


def arrange(idx, w):
    return call(
        arrange_kernel,
        jax.ShapeDtypeStruct((2, 1536, 768), BF16),
        [SMEM, HBM],
        HBM,
        [pltpu.SemaphoreType.DMA((16,))],
        0,
        10 << 20,
    )(idx, w)


def join_kernel(n, *refs):
    *ins, out, sems = refs
    copies = []
    for i, a in enumerate(ins):
        copies.append(pltpu.make_async_copy(a, out.at[pl.ds(i * n, n), :], sems.at[i]))
    run_copies(copies)


def join(*values):
    rows, width = values[0].shape
    return call(
        functools.partial(join_kernel, rows),
        jax.ShapeDtypeStruct((len(values) * rows, width), BF16),
        [HBM] * len(values),
        HBM,
        [pltpu.SemaphoreType.DMA((len(values),))],
        0,
        4 * len(values) * rows * width,
    )(*values)


def across(a, w):
    return lax.dot_general(a, w, (((0,), (0,)), ((), ())), preferred_element_type=F32)


def turn_of(idx):
    return idx[0] ^ (idx[2] >> 1)


def first_kernel(idx, a, w, out):
    for rel in range(2):
        out[rel] = across(a[rel ^ turn_of(idx)], w[0])


def second_kernel(idx, acc, a, w, mine, theirs):
    for rel, out in ((1, theirs), (0, mine)):
        out[...] = (acc[rel] + across(a[rel ^ turn_of(idx)], w[1])).astype(out.dtype)


def project_first(idx, a_own, w_rel, width):
    return call(
        first_kernel,
        jax.ShapeDtypeStruct((2, width, 768), F32),
        [SMEM, VMEM, VMEM],
        VMEM,
        [],
        8 * width * 768 * 768,
        20 * 1024 * width,
    )(idx, a_own.reshape(2, 1536, width), w_rel)


def project_second(idx, acc, a_other, w_rel, width):
    return call(
        second_kernel,
        [jax.ShapeDtypeStruct((width, 768), F32), jax.ShapeDtypeStruct((width, 768), BF16)],
        [SMEM, VMEM, VMEM, VMEM],
        [VMEM] * 2,
        [],
        8 * width * 768 * 768,
        20 * 1024 * width,
    )(idx, acc, a_other.reshape(2, 1536, width), w_rel)


def input_grad_kernel(which, idx, g0, g1, w, out):
    for rel, g in enumerate((g0, g1)):
        block = rel ^ turn_of(idx)
        part = lax.dot_general(
            w[which], g[...], (((1,), (1,)), ((), ())), preferred_element_type=F32
        ).astype(BF16)
        for near in range(2):
            out[block * 2 + (near ^ block)] = part[near * 768 : near * 768 + 768]


def input_grad(idx, grads, w_rel, which, width):
    return call(
        functools.partial(input_grad_kernel, which),
        jax.ShapeDtypeStruct((4, 768, width), BF16),
        [SMEM] + [VMEM] * 3,
        VMEM,
        [],
        8 * width * 768 * 768,
        20 * 1024 * width,
    )(idx, *grads, w_rel)


def weight_grad_kernel(count, idx, *refs):
    grads, gathered, out = refs[: 2 * count], refs[2 * count : 4 * count], refs[4 * count]
    for dc in range(2):
        for near in range(2):
            total = None
            for i in range(count):
                a = gathered[2 * i + dc]
                for rel in range(2):
                    term = jnp.dot(
                        a[rel ^ turn_of(idx), near * 768 : near * 768 + 768, :],
                        grads[2 * i + rel][...],
                        preferred_element_type=F32,
                    )
                    total = term if total is None else total + term
            total = total.astype(BF16)
            for dz in range(4):
                out[pl.ds(weight_row(idx, near, dz, dc), 192), :] = total[dz * 192 : dz * 192 + 192]


def weight_grad(idx, grads, gathered):
    count = len(grads) // 2
    width = grads[0].shape[0]
    return call(
        functools.partial(weight_grad_kernel, count),
        jax.ShapeDtypeStruct((3072, 768), BF16),
        [SMEM] + [VMEM] * (4 * count),
        VMEM,
        [],
        8 * count * width * 1536 * 768,
        16 << 20,
    )(idx, *grads, *[a.reshape(2, 1536, width) for a in gathered])


def gelu_pair(pre_act, grad_out):
    inside = slope_coef * (pre_act + 0.044715 * pre_act * pre_act * pre_act)
    tangent = jnp.tanh(inside)
    activated = 0.5 * pre_act * (1.0 + tangent)
    slope = 0.5 * (1.0 + tangent) + 0.5 * pre_act * (1.0 - tangent * tangent) * slope_coef * (
        1.0 + 3.0 * 0.044715 * pre_act * pre_act
    )
    return activated.astype(BF16), (grad_out.astype(F32) * slope).astype(BF16)


def stage(*values):
    return lax.optimization_barrier(values)


def added(first, others):
    total = first.astype(F32)
    for other in others:
        total = total + other.astype(F32)
    return total


def gather_pieces(value, axis):
    return [value] + [flip(value, axis, d) for d in (1, 2, 3)]


def in_order(planes):
    return join(planes[0], planes[1], planes[3], planes[2])


def per_device(tokens, weight, grad_out):
    idx = jnp.stack([lax.axis_index(axis) for axis in AXES]).astype(jnp.int32)
    n = 256
    w_all = lax.all_gather(weight, "x", axis=0, tiled=True)
    w_rel = arrange(idx, w_all)
    piece = spread(tokens.T)
    piece_a, piece_b = piece[:, :n], piece[:, n:]
    *pieces_a, piece_b = stage(*gather_pieces(piece_a, "zh"), piece_b)

    pieces_b = gather_pieces(piece_b, "zh")
    planes_a = gather_pieces(join(*pieces_a), "y")
    stages = stage(*planes_a, *pieces_b)
    planes_a, pieces_b = stages[:4], stages[4:]

    own_a = in_order(planes_a)
    planes_b = gather_pieces(join(*pieces_b), "y")
    other_a = flip(own_a, "c", 1)
    acc = project_first(idx, own_a, w_rel, n)
    p_a, send = project_second(idx, acc, other_a, w_rel, n)
    *planes_b, came_a = stage(*planes_b, over_z(send))

    own_b = in_order(planes_b)
    act_a, grad_a = gelu_pair(added(p_a, [came_a]), grad_out[:n])
    other_b = flip(own_b, "c", 1)
    acc = project_first(idx, own_b, w_rel, n)
    p_b, send = project_second(idx, acc, other_b, w_rel, n)
    grad_a2, send = stage(over_z(grad_a), send)

    all_a = [grad_a, grad_a2]
    came_b = over_z(send)
    half = flip(input_grad(idx, all_a, w_rel, 1, n), "c", 1)
    both_a = added(input_grad(idx, all_a, w_rel, 0, n), [half]).astype(BF16)
    came_b, both_a = stage(came_b, both_a)

    act_b, grad_b = gelu_pair(added(p_b, [came_b]), grad_out[n:])
    grad_b2, *rows_a = stage(over_z(grad_b), *[flip(both_a[d], "y", d) for d in (1, 2, 3)])

    all_b = [grad_b, grad_b2]
    half = flip(input_grad(idx, all_b, w_rel, 1, n), "c", 1)
    partial = weight_grad(idx, all_a + all_b, [own_a, other_a, own_b, other_b])
    grad_weight = lax.psum_scatter(partial, "x", scatter_dimension=0, tiled=True)
    both_b = added(input_grad(idx, all_b, w_rel, 0, n), [half]).astype(BF16)
    line_a = added(both_a[0], rows_a).astype(BF16).reshape(4, 192, n)
    both_b, line_a = stage(both_b, line_a)

    rows_b = [flip(both_b[d], "y", d) for d in (1, 2, 3)]
    homes_a = [flip(line_a[d], "zh", d) for d in (1, 2, 3)]
    stages = stage(*rows_b, *homes_a)
    rows_b, homes_a = stages[:3], stages[3:]

    line_b = added(both_b[0], rows_b).astype(BF16).reshape(4, 192, n)
    homes_b = [flip(line_b[d], "zh", d) for d in (1, 2, 3)]
    final_a = spread_back(added(line_a[0], homes_a).astype(BF16))
    *homes_b, final_a = stage(*homes_b, final_a)
    final_b = spread_back(added(line_b[0], homes_b).astype(BF16))
    grad_tokens = jnp.concatenate([final_a, final_b], axis=1).T
    return jnp.concatenate([act_a, act_b], axis=0), grad_tokens, grad_weight


def solution(mesh):
    fine = Mesh(mesh.devices.reshape(2, 4, 4, 4, 2), AXES)
    spec = P(("zl", "x"), ("y", "zh", "c"))
    return jax.shard_map(
        per_device, mesh=fine, in_specs=(spec,) * 3, out_specs=(spec,) * 3, check_vma=False
    )
```

time: 431 us -> 214 us (0.50)
  waiting for transfers between devices: 381 us -> 79.4 us
  starting transfers between devices: 0.16 us -> 76.3 us
  matrix products: 31.8 us -> 0 us
  Pallas kernels: 0 us -> 27 us
  local copies, waits for them, and re-layouts: 2.38 us -> 10.8 us
  other arithmetic: 0 us -> 5.35 us
    reduce_scatter x2 -> x1, waiting for transfers between devices: 205 us -> 0.01 us  [per_device(): lax.psum_scatter(partial, 'x', scatter_dimension=0, tiled=True)]
    all_gather x2 -> x1, waiting for transfers between devices: 175 us -> 0.73 us  [per_device(): w_all = lax.all_gather(weight, 'x', axis=0, tiled=True)]
    ppermute x0 -> x35, waiting for transfers between devices: none -> 77.9 us  [the longest x32 64.4 us: flip(): lax.ppermute(value, axis, [(i, i ^ mask) for i in range(SIZES[axis])])]
    ppermute x0 -> x35, starting transfers between devices: none -> 76.2 us  [the longest x32 65.6 us: flip(): lax.ppermute(value, axis, [(i, i ^ mask) for i in range(SIZES[axis])])]
    dot_general x3 -> x0, matrix products: 31.8 us -> none  [the longest x1 11.3 us: per_device(): lax.dot_general(grad_pre, lax.all_gather(weight, 'row', axis=0, tiled=Tru...]
    pallas_call x0 -> x14, Pallas kernels: none -> 27 us  [the longest x4 8.12 us: input_grad(): call(functools.partial(input_grad_kernel, which), jax.ShapeDtypeStruct((4...]
    unnamed x5 -> x40, local copies, waits for them, and re-layouts: 2.38 us -> 10.5 us
  transfers between devices with their start and end apart: 4 -> 37, of which waited for: 4 -> 25; matrix products, arithmetic and copies ran while one was open for 3% -> 2% of each run, Pallas kernels for 0% -> 8%
where the time goes in v1:
time: 214 us; the launch traced here: 213 us
  waiting for transfers between devices  79.4 us (37%)
  starting transfers between devices  76.3 us (36%)
  Pallas kernels  27 us (13%)
  between operations  14.5 us (7%)
  local copies, waits for them, and re-layouts  10.8 us (5%)
  other arithmetic  5.35 us (2%)
    ppermute x32, starting transfers between devices, flip(): lax.ppermute(value, axis, [(i, i ^ mask) for i in range(SIZES[axis])])  65.6 us
    ppermute x32, waiting for transfers between devices, flip(): lax.ppermute(value, axis, [(i, i ^ mask) for i in range(SIZES[axis])])  64.4 us
    unnamed x40, local copies, waits for them, and re-layouts  10.5 us
    pallas_call x4, Pallas kernels, input_grad(): call(functools.partial(input_grad_kernel, which), jax.ShapeDtypeStruct((4...  8.12 us
    ppermute x2, waiting for transfers between devices, spread_back(): return lax.ppermute(value, ('zl', 'y'), [(b, a) for a, b in spread_pairs()])  7.18 us
    ppermute x1, waiting for transfers between devices, spread(): return lax.ppermute(value, ('zl', 'y'), spread_pairs())  6.38 us
    ppermute x2, starting transfers between devices, spread_back(): return lax.ppermute(value, ('zl', 'y'), [(b, a) for a, b in spread_pairs()])  6.14 us
    pallas_call x1, Pallas kernels, weight_grad(): call(functools.partial(weight_grad_kernel, count), jax.ShapeDtypeStruct((...  6.04 us
  transfers between devices with their start and end apart: 37, of which 25 were waited for; matrix products, arithmetic and copies ran while one was open for 2% of the time, Pallas kernels for 8%

profile of v1, /device:TPU:38, one launch (start us, length us, event | category | flops | bytes accessed | tf_op | source)
XLA Modules:
  0.0 213.2 jit_solution(11067942494744250885)
XLA Ops:
  7.9 4.5 %collective-permute-start = (bf16[192,512]{1,0:T(8,128)(2,1)}, bf16[192,512]{1,0:T(8,128)(2,1)S(1)}, u32[]{:S(2)}, u32[]{:S(2)}) collective-permute-start(bf16[192,512]{1,0:T(8,128)(2,1)} %bitcast.50), channel_id=1, source_target_pairs={{0,0},{8,8},{16,136},{24,128},{128,24},{136,16},{144,144},{152,152... | collective-permute-start | bytes 589832 | tf_op jit(solution)/shard_map/ppermute | solution.py:40
  12.4 6.4 %collective-permute-done = bf16[192,512]{1,0:T(8,128)(2,1)S(1)} collective-permute-done((bf16[192,512]{1,0:T(8,128)(2,1)}, bf16[192,512]{1,0:T(8,128)(2,1)S(1)}, u32[]{:S(2)}, u32[]{:S(2)}) %collective-permute-start) | collective-permute-done | bytes 196640 | tf_op jit(solution)/shard_map/ppermute | solution.py:40
  18.8 5.5 %collective-permute-start.1 = (bf16[192,256]{1,0:T(8,128)(2,1)S(1)}, bf16[192,256]{1,0:T(8,128)(2,1)S(1)}, u32[]{:S(2)}, u32[]{:S(2)}) collective-permute-start(bf16[192,256]{1,0:T(8,128)(2,1)S(1)} %get-tuple-element.45.refs_0_), channel_id=1, source_target_pairs={{0,2},{2,0},{4,6},{6,4},{1,3},{3,1},{5,7},{7,5},{8,10},{10,8},{12,... | collective-permute-start | bytes 294920 | tf_op jit(solution)/shard_map/ppermute | solution.py:23
  24.3 4.5 %collective-permute-start.2 = (bf16[192,256]{1,0:T(8,128)(2,1)S(1)}, bf16[192,256]{1,0:T(8,128)(2,1)S(1)}, u32[]{:S(2)}, u32[]{:S(2)}) collective-permute-start(bf16[192,256]{1,0:T(8,128)(2,1)S(1)} %get-tuple-element.45.refs_0_), channel_id=1, source_target_pairs={{0,4},{2,6},{4,0},{6,2},{1,5},{3,7},{5,1},{7,3},{8,12},{10,14},{12... | collective-permute-start | bytes 294920 | tf_op jit(solution)/shard_map/ppermute | solution.py:23
  28.8 6.0 %collective-permute-done.2.refs_2_ = bf16[192,256]{1,0:T(8,128)(2,1)S(1)} collective-permute-done((bf16[192,256]{1,0:T(8,128)(2,1)S(1)}, bf16[192,256]{1,0:T(8,128)(2,1)S(1)}, u32[]{:S(2)}, u32[]{:S(2)}) %collective-permute-start.2) | collective-permute-done | bytes 98336 | tf_op jit(solution)/shard_map/ppermute | solution.py:23
  36.5 4.3 %collective-permute-start.6 = (bf16[768,256]{1,0:T(8,128)(2,1)S(1)}, bf16[768,256]{1,0:T(8,128)(2,1)S(1)}, u32[]{:S(2)}, u32[]{:S(2)}) collective-permute-start(bf16[768,256]{1,0:T(8,128)(2,1)S(1)} %shard_map.58.refs_0_), channel_id=1, source_target_pairs={{0,24},{8,16},{16,8},{24,0},{1,25},{9,17},{17,9},{25,1},{2,26},{10... | collective-permute-start | bytes 1179656 | tf_op jit(solution)/shard_map/ppermute | solution.py:23
  41.7 4.5 %collective-permute-start.8 = (bf16[192,256]{1,0:T(8,128)(2,1)S(1)}, bf16[192,256]{1,0:T(8,128)(2,1)S(1)}, u32[]{:S(2)}, u32[]{:S(2)}) collective-permute-start(bf16[192,256]{1,0:T(8,128)(2,1)S(1)} %get-tuple-element.55.refs_0_), channel_id=1, source_target_pairs={{0,4},{2,6},{4,0},{6,2},{1,5},{3,7},{5,1},{7,3},{8,12},{10,14},{12... | collective-permute-start | bytes 294920 | tf_op jit(solution)/shard_map/ppermute | solution.py:23
  47.0 4.2 %collective-permute-start.9 = (bf16[192,256]{1,0:T(8,128)(2,1)S(1)}, bf16[192,256]{1,0:T(8,128)(2,1)S(1)}, u32[]{:S(2)}, u32[]{:S(2)}) collective-permute-start(bf16[192,256]{1,0:T(8,128)(2,1)S(1)} %get-tuple-element.55.refs_0_), channel_id=1, source_target_pairs={{0,6},{2,4},{4,2},{6,0},{1,7},{3,5},{5,3},{7,1},{8,14},{10,12},{12... | collective-permute-start | bytes 294920 | tf_op jit(solution)/shard_map/ppermute | solution.py:23
  51.7 2.4 %collective-permute-done.9.refs_3_ = bf16[192,256]{1,0:T(8,128)(2,1)S(1)} collective-permute-done((bf16[192,256]{1,0:T(8,128)(2,1)S(1)}, bf16[192,256]{1,0:T(8,128)(2,1)S(1)}, u32[]{:S(2)}, u32[]{:S(2)}) %collective-permute-start.9) | collective-permute-done | bytes 98336 | tf_op jit(solution)/shard_map/ppermute | solution.py:23
  60.5 4.9 %collective-permute-start.12 = (bf16[768,256]{1,0:T(8,128)(2,1)S(1)}, bf16[768,256]{1,0:T(8,128)(2,1)}, u32[]{:S(2)}, u32[]{:S(2)}) collective-permute-start(bf16[768,256]{1,0:T(8,128)(2,1)S(1)} %shard_map.63.refs_0_), channel_id=1, source_target_pairs={{0,16},{8,24},{16,0},{24,8},{1,17},{9,25},{17,1},{25,9},{2,18},{10... | collective-permute-start | bytes 1179656 | tf_op jit(solution)/shard_map/ppermute | solution.py:23
  66.1 2.3 %copy-done.3 = bf16[3072,768]{1,0:T(8,128)(2,1)S(1)} copy-done((bf16[3072,768]{1,0:T(8,128)(2,1)S(1)}, bf16[3072,768]{1,0:T(8,128)(2,1)}, u32[]{:S(2)}) %copy-start.3) | copy-done | bytes 4718616
  70.2 1.9 shard_map.61.acc
  72.1 2.0 shard_map.62
  74.1 3.9 %collective-permute-start.14 = (bf16[256,768]{1,0:T(8,128)(2,1)S(1)}, bf16[256,768]{1,0:T(8,128)(2,1)S(1)}, u32[]{:S(2)}, u32[]{:S(2)}) collective-permute-start(bf16[256,768]{1,0:T(8,128)(2,1)S(1)} %get-tuple-element.59), channel_id=1, source_target_pairs={{0,128},{128,0},{1,129},{129,1},{2,130},{130,2},{3,131},{131,3},{4... | collective-permute-start | bytes 1179656 | tf_op jit(solution)/shard_map/ppermute | solution.py:23
  78.1 5.4 %collective-permute-done.12.refs_3_ = bf16[768,256]{1,0:T(8,128)(2,1)} collective-permute-done((bf16[768,256]{1,0:T(8,128)(2,1)S(1)}, bf16[768,256]{1,0:T(8,128)(2,1)}, u32[]{:S(2)}, u32[]{:S(2)}) %collective-permute-start.12) | collective-permute-done | bytes 393248 | tf_op jit(solution)/shard_map/ppermute | solution.py:23
  83.5 2.6 %collective-permute-done.13.refs_2_ = bf16[768,256]{1,0:T(8,128)(2,1)} collective-permute-done((bf16[768,256]{1,0:T(8,128)(2,1)S(1)}, bf16[768,256]{1,0:T(8,128)(2,1)}, u32[]{:S(2)}, u32[]{:S(2)}) %collective-permute-start.13) | collective-permute-done | bytes 393248 | tf_op jit(solution)/shard_map/ppermute | solution.py:23
  89.4 1.8 collective-permute-start.16
  91.2 1.9 shard_map.65.acc
  93.2 2.0 shard_map.66
  95.1 5.8 %collective-permute-done.16.g1.refs_1_ = bf16[256,768]{1,0:T(8,128)(2,1)S(1)} collective-permute-done((bf16[256,768]{1,0:T(8,128)(2,1)S(1)}, bf16[256,768]{1,0:T(8,128)(2,1)S(1)}, u32[]{:S(2)}, u32[]{:S(2)}) %collective-permute-start.16) | collective-permute-done | bytes 393248 | tf_op jit(solution)/shard_map/ppermute | solution.py:23
  101.0 2.0 shard_map.68
  103.1 1.8 collective-permute-start.17
  104.9 2.0 shard_map.67
  107.4 7.2 %collective-permute-done.17 = bf16[256,768]{1,0:T(8,128)(2,1)S(1)} collective-permute-done((bf16[256,768]{1,0:T(8,128)(2,1)S(1)}, bf16[256,768]{1,0:T(8,128)(2,1)S(1)}, u32[]{:S(2)}, u32[]{:S(2)}) %collective-permute-start.17) | collective-permute-done | bytes 393248 | tf_op jit(solution)/shard_map/ppermute | solution.py:23
  115.3 1.8 collective-permute-start.19
  117.3 3.3 %collective-permute-start.21 = (bf16[768,256]{1,0:T(8,128)(2,1)S(1)}, bf16[768,256]{1,0:T(8,128)(2,1)S(1)}, u32[]{:S(2)}, u32[]{:S(2)}) collective-permute-start(bf16[768,256]{1,0:T(8,128)(2,1)S(1)} %get-tuple-element.91), channel_id=1, source_target_pairs={{0,16},{8,24},{16,0},{24,8},{1,17},{9,25},{17,1},{25,9},{2,18},{10... | collective-permute-start | bytes 1179656 | tf_op jit(solution)/shard_map/ppermute | solution.py:23
  122.0 4.0 %collective-permute-done.19.g1.refs_3_ = bf16[256,768]{1,0:T(8,128)(2,1)S(1)} collective-permute-done((bf16[256,768]{1,0:T(8,128)(2,1)S(1)}, bf16[256,768]{1,0:T(8,128)(2,1)S(1)}, u32[]{:S(2)}, u32[]{:S(2)}) %collective-permute-start.19) | collective-permute-done | bytes 393248 | tf_op jit(solution)/shard_map/ppermute | solution.py:23
  126.0 3.3 %collective-permute-done.20 = bf16[768,256]{1,0:T(8,128)(2,1)S(1)} collective-permute-done((bf16[768,256]{1,0:T(8,128)(2,1)S(1)}, bf16[768,256]{1,0:T(8,128)(2,1)S(1)}, u32[]{:S(2)}, u32[]{:S(2)}) %collective-permute-start.20) | collective-permute-done | bytes 393248 | tf_op jit(solution)/shard_map/ppermute | solution.py:23
  129.4 8.2 %collective-permute-done.21 = bf16[768,256]{1,0:T(8,128)(2,1)S(1)} collective-permute-done((bf16[768,256]{1,0:T(8,128)(2,1)S(1)}, bf16[768,256]{1,0:T(8,128)(2,1)S(1)}, u32[]{:S(2)}, u32[]{:S(2)}) %collective-permute-start.21) | collective-permute-done | bytes 393248 | tf_op jit(solution)/shard_map/ppermute | solution.py:23
  137.5 2.7 %collective-permute-done.22 = bf16[768,256]{1,0:T(8,128)(2,1)} collective-permute-done((bf16[768,256]{1,0:T(8,128)(2,1)S(1)}, bf16[768,256]{1,0:T(8,128)(2,1)}, u32[]{:S(2)}, u32[]{:S(2)}) %collective-permute-start.22) | collective-permute-done | bytes 393248 | tf_op jit(solution)/shard_map/ppermute | solution.py:23
  140.2 6.0 %shard_map.71 = bf16[3072,768]{1,0:T(8,128)(2,1)S(1)} custom-call(s32[5]{0:T(128)S(1)} %stack.23.idx, bf16[256,768]{1,0:T(8,128)(2,1)S(1)} %get-tuple-element.96.g0.refs_0_, bf16[256,768]{1,0:T(8,128)(2,1)S(1)} %collective-permute-done.16.g1.refs_1_, bf16[256,768]{1,0:T(8,128)(2,1)S(1)} %get-tuple-element.93.g0.refs_2_, ...), custom_call_target="tpu_custom_call" | custom-call | flops 4831838208 | bytes 16777216 | tf_op jit(solution)/shard_map/pallas_call | solution.py:206
  146.3 2.2 %copy-done.2 = bf16[3072,768]{1,0:T(8,128)(2,1)} copy-done((bf16[3072,768]{1,0:T(8,128)(2,1)}, bf16[3072,768]{1,0:T(8,128)(2,1)S(1)}, u32[]{:S(2)}) %copy-start.2) | copy-done | bytes 4718616
  148.5 2.3 %copy-done.1 = bf16[2,1536,768]{2,1,0:T(8,128)(2,1)S(1)} copy-done((bf16[2,1536,768]{2,1,0:T(8,128)(2,1)S(1)}, bf16[2,1536,768]{2,1,0:T(8,128)(2,1)}, u32[]{:S(2)}) %copy-start.1) | copy-done | bytes 4718616
  150.8 2.0 shard_map.70
  153.0 2.0 shard_map.69
  156.9 2.8 %collective-permute-start.25 = (bf16[768,256]{1,0:T(8,128)(2,1)S(1)}, bf16[768,256]{1,0:T(8,128)(2,1)S(1)}, u32[]{:S(2)}, u32[]{:S(2)}) collective-permute-start(bf16[768,256]{1,0:T(8,128)(2,1)S(1)} %get-tuple-element.88), channel_id=1, source_target_pairs={{0,16},{8,24},{16,0},{24,8},{1,17},{9,25},{17,1},{25,9},{2,18},{10... | collective-permute-start | bytes 1179656 | tf_op jit(solution)/shard_map/ppermute | solution.py:23
  159.7 1.9 collective-permute-start.26
  161.9 3.9 %collective-permute-start.28 = (bf16[192,256]{1,0:T(8,128)(2,1)S(1)}, bf16[192,256]{1,0:T(8,128)(2,1)S(1)}, u32[]{:S(2)}, u32[]{:S(2)}) collective-permute-start(bf16[192,256]{1,0:T(8,128)(2,1)S(1)} %get-tuple-element.101), channel_id=1, source_target_pairs={{0,4},{2,6},{4,0},{6,2},{1,5},{3,7},{5,1},{7,3},{8,12},{10,14},{12... | collective-permute-start | bytes 294920 | tf_op jit(solution)/shard_map/ppermute | solution.py:23
  167.3 5.8 %collective-permute-start.29 = (bf16[192,256]{1,0:T(8,128)(2,1)S(1)}, bf16[192,256]{1,0:T(8,128)(2,1)S(1)}, u32[]{:S(2)}, u32[]{:S(2)}) collective-permute-start(bf16[192,256]{1,0:T(8,128)(2,1)S(1)} %get-tuple-element.100), channel_id=1, source_target_pairs={{0,6},{2,4},{4,2},{6,0},{1,7},{3,5},{5,3},{7,1},{8,14},{10,12},{12... | collective-permute-start | bytes 294920 | tf_op jit(solution)/shard_map/ppermute | solution.py:23
  173.1 4.6 %collective-permute-done.29 = bf16[192,256]{1,0:T(8,128)(2,1)S(1)} collective-permute-done((bf16[192,256]{1,0:T(8,128)(2,1)S(1)}, bf16[192,256]{1,0:T(8,128)(2,1)S(1)}, u32[]{:S(2)}, u32[]{:S(2)}) %collective-permute-start.29) | collective-permute-done | bytes 98336 | tf_op jit(solution)/shard_map/ppermute | solution.py:23
  177.8 2.6 %collective-permute-done.26 = bf16[768,256]{1,0:T(8,128)(2,1)S(1)} collective-permute-done((bf16[768,256]{1,0:T(8,128)(2,1)S(1)}, bf16[768,256]{1,0:T(8,128)(2,1)S(1)}, u32[]{:S(2)}, u32[]{:S(2)}) %collective-permute-start.26) | collective-permute-done | bytes 393248 | tf_op jit(solution)/shard_map/ppermute | solution.py:23
  180.7 4.0 %collective-permute-start.31 = (bf16[192,256]{1,0:T(8,128)(2,1)S(1)}, bf16[192,256]{1,0:T(8,128)(2,1)S(1)}, u32[]{:S(2)}, u32[]{:S(2)}) collective-permute-start(bf16[192,256]{1,0:T(8,128)(2,1)S(1)} %get-tuple-element.98), channel_id=1, source_target_pairs={{0,4},{2,6},{4,0},{6,2},{1,5},{3,7},{5,1},{7,3},{8,12},{10,14},{12... | collective-permute-start | bytes 294920 | tf_op jit(solution)/shard_map/ppermute | solution.py:23
  184.7 2.5 %collective-permute-start.32 = (bf16[192,256]{1,0:T(8,128)(2,1)S(1)}, bf16[192,256]{1,0:T(8,128)(2,1)S(1)}, u32[]{:S(2)}, u32[]{:S(2)}) collective-permute-start(bf16[192,256]{1,0:T(8,128)(2,1)S(1)} %get-tuple-element.97), channel_id=1, source_target_pairs={{0,6},{2,4},{4,2},{6,0},{1,7},{3,5},{5,3},{7,1},{8,14},{10,12},{12... | collective-permute-start | bytes 294920 | tf_op jit(solution)/shard_map/ppermute | solution.py:23
  187.2 3.5 %collective-permute-start.33 = (bf16[192,256]{1,0:T(8,128)(2,1)S(1)}, bf16[192,256]{1,0:T(8,128)(2,1)S(1)}, u32[]{:S(2)}, u32[]{:S(2)}) collective-permute-start(bf16[192,256]{1,0:T(8,128)(2,1)S(1)} %fusion.22), channel_id=1, source_target_pairs={{0,0},{8,8},{136,16},{128,24},{24,128},{16,136},{144,144},{152,152... | collective-permute-start | bytes 294920 | tf_op jit(solution)/shard_map/ppermute | solution.py:44
  190.8 4.1 %collective-permute-done.32 = bf16[192,256]{1,0:T(8,128)(2,1)S(1)} collective-permute-done((bf16[192,256]{1,0:T(8,128)(2,1)S(1)}, bf16[192,256]{1,0:T(8,128)(2,1)S(1)}, u32[]{:S(2)}, u32[]{:S(2)}) %collective-permute-start.32) | collective-permute-done | bytes 98336 | tf_op jit(solution)/shard_map/ppermute | solution.py:23
  194.9 2.1 collective-permute-done.33
  197.0 2.6 %collective-permute-start.34 = (bf16[192,256]{1,0:T(8,128)(2,1)S(1)}, bf16[192,256]{1,0:T(8,128)(2,1)S(1)}, u32[]{:S(2)}, u32[]{:S(2)}) collective-permute-start(bf16[192,256]{1,0:T(8,128)(2,1)S(1)} %add_convert_fusion.2), channel_id=1, source_target_pairs={{0,0},{8,8},{136,16},{128,24},{24,128},{16,136},{144,144},{152,152... | collective-permute-start | bytes 294920 | tf_op jit(solution)/shard_map/ppermute | solution.py:44
  200.6 5.1 %collective-permute-done.34 = bf16[192,256]{1,0:T(8,128)(2,1)S(1)} collective-permute-done((bf16[192,256]{1,0:T(8,128)(2,1)S(1)}, bf16[192,256]{1,0:T(8,128)(2,1)S(1)}, u32[]{:S(2)}, u32[]{:S(2)}) %collective-permute-start.34) | collective-permute-done | bytes 98336 | tf_op jit(solution)/shard_map/ppermute | solution.py:44
  (98 shorter events, 25.3 us)
Async XLA Ops:
  7.2 58.9 %all-gather.2.cloned.1.call-start = ((), (), s32[]{:S(2)}) async-start(), calls=%async_computation.1 | async-start | bytes 5898240 | tf_op jit(solution)/shard_map/all_gather | solution.py:249
  7.9 198.4 %reduce-scatter.2.cloned.1.call-start = ((), (), s32[]{:S(2)}) async-start(), calls=%async_computation.2 | async-start | bytes 5898240 | tf_op jit(solution)/shard_map/reduce_scatter | solution.py:286
  7.9 10.9 %collective-permute-start = (bf16[192,512]{1,0:T(8,128)(2,1)}, bf16[192,512]{1,0:T(8,128)(2,1)S(1)}, u32[]{:S(2)}, u32[]{:S(2)}) collective-permute-start(bf16[192,512]{1,0:T(8,128)(2,1)} %bitcast.50), channel_id=1, source_target_pairs={{0,0},{8,8},{16,136},{24,128},{128,24},{136,16},{144,144},{152,152... | collective-permute-start | bytes 589832 | tf_op jit(solution)/shard_map/ppermute | solution.py:40
  18.8 37.1 %copy-start.6 = (bf16[192,256]{1,0:T(8,128)(2,1)}, bf16[192,256]{1,0:T(8,128)(2,1)S(1)}, u32[]{:S(2)}) copy-start(bf16[192,256]{1,0:T(8,128)(2,1)S(1)} %get-tuple-element.55.refs_0_) | copy-start | bytes 294916
  18.8 10.0 %collective-permute-start.1 = (bf16[192,256]{1,0:T(8,128)(2,1)S(1)}, bf16[192,256]{1,0:T(8,128)(2,1)S(1)}, u32[]{:S(2)}, u32[]{:S(2)}) collective-permute-start(bf16[192,256]{1,0:T(8,128)(2,1)S(1)} %get-tuple-element.45.refs_0_), channel_id=1, source_target_pairs={{0,2},{2,0},{4,6},{6,4},{1,3},{3,1},{5,7},{7,5},{8,10},{10,8},{12,... | collective-permute-start | bytes 294920 | tf_op jit(solution)/shard_map/ppermute | solution.py:23
  24.3 10.5 %collective-permute-start.2 = (bf16[192,256]{1,0:T(8,128)(2,1)S(1)}, bf16[192,256]{1,0:T(8,128)(2,1)S(1)}, u32[]{:S(2)}, u32[]{:S(2)}) collective-permute-start(bf16[192,256]{1,0:T(8,128)(2,1)S(1)} %get-tuple-element.45.refs_0_), channel_id=1, source_target_pairs={{0,4},{2,6},{4,0},{6,2},{1,5},{3,7},{5,1},{7,3},{8,12},{10,14},{12... | collective-permute-start | bytes 294920 | tf_op jit(solution)/shard_map/ppermute | solution.py:23
  28.8 6.7 %collective-permute-start.3 = (bf16[192,256]{1,0:T(8,128)(2,1)S(1)}, bf16[192,256]{1,0:T(8,128)(2,1)S(1)}, u32[]{:S(2)}, u32[]{:S(2)}) collective-permute-start(bf16[192,256]{1,0:T(8,128)(2,1)S(1)} %get-tuple-element.45.refs_0_), channel_id=1, source_target_pairs={{0,6},{2,4},{4,2},{6,0},{1,7},{3,5},{5,3},{7,1},{8,14},{10,12},{12... | collective-permute-start | bytes 294920 | tf_op jit(solution)/shard_map/ppermute | solution.py:23
  36.0 18.1 %collective-permute-start.4 = (bf16[768,256]{1,0:T(8,128)(2,1)S(1)}, bf16[768,256]{1,0:T(8,128)(2,1)S(1)}, u32[]{:S(2)}, u32[]{:S(2)}) collective-permute-start(bf16[768,256]{1,0:T(8,128)(2,1)S(1)} %shard_map.58.refs_0_), channel_id=1, source_target_pairs={{0,8},{8,0},{16,24},{24,16},{1,9},{9,1},{17,25},{25,17},{2,10},{10... | collective-permute-start | bytes 1179656 | tf_op jit(solution)/shard_map/ppermute | solution.py:23
  36.5 17.7 %collective-permute-start.5 = (bf16[768,256]{1,0:T(8,128)(2,1)S(1)}, bf16[768,256]{1,0:T(8,128)(2,1)S(1)}, u32[]{:S(2)}, u32[]{:S(2)}) collective-permute-start(bf16[768,256]{1,0:T(8,128)(2,1)S(1)} %shard_map.58.refs_0_), channel_id=1, source_target_pairs={{0,16},{8,24},{16,0},{24,8},{1,17},{9,25},{17,1},{25,9},{2,18},{10... | collective-permute-start | bytes 1179656 | tf_op jit(solution)/shard_map/ppermute | solution.py:23
  36.5 18.6 %collective-permute-start.6 = (bf16[768,256]{1,0:T(8,128)(2,1)S(1)}, bf16[768,256]{1,0:T(8,128)(2,1)S(1)}, u32[]{:S(2)}, u32[]{:S(2)}) collective-permute-start(bf16[768,256]{1,0:T(8,128)(2,1)S(1)} %shard_map.58.refs_0_), channel_id=1, source_target_pairs={{0,24},{8,16},{16,8},{24,0},{1,25},{9,17},{17,9},{25,1},{2,26},{10... | collective-permute-start | bytes 1179656 | tf_op jit(solution)/shard_map/ppermute | solution.py:23
  40.8 6.2 %collective-permute-start.7 = (bf16[192,256]{1,0:T(8,128)(2,1)S(1)}, bf16[192,256]{1,0:T(8,128)(2,1)S(1)}, u32[]{:S(2)}, u32[]{:S(2)}) collective-permute-start(bf16[192,256]{1,0:T(8,128)(2,1)S(1)} %get-tuple-element.55.refs_0_), channel_id=1, source_target_pairs={{0,2},{2,0},{4,6},{6,4},{1,3},{3,1},{5,7},{7,5},{8,10},{10,8},{12,... | collective-permute-start | bytes 294920 | tf_op jit(solution)/shard_map/ppermute | solution.py:23
  41.7 10.0 %collective-permute-start.8 = (bf16[192,256]{1,0:T(8,128)(2,1)S(1)}, bf16[192,256]{1,0:T(8,128)(2,1)S(1)}, u32[]{:S(2)}, u32[]{:S(2)}) collective-permute-start(bf16[192,256]{1,0:T(8,128)(2,1)S(1)} %get-tuple-element.55.refs_0_), channel_id=1, source_target_pairs={{0,4},{2,6},{4,0},{6,2},{1,5},{3,7},{5,1},{7,3},{8,12},{10,14},{12... | collective-permute-start | bytes 294920 | tf_op jit(solution)/shard_map/ppermute | solution.py:23
  47.0 8.9 %copy-start.8 = (bf16[192,256]{1,0:T(8,128)(2,1)}, bf16[192,256]{1,0:T(8,128)(2,1)S(1)}, u32[]{:S(2)}) copy-start(bf16[192,256]{1,0:T(8,128)(2,1)S(1)} %collective-permute-done.7.refs_1_) | copy-start | bytes 294916
  47.0 7.1 %collective-permute-start.9 = (bf16[192,256]{1,0:T(8,128)(2,1)S(1)}, bf16[192,256]{1,0:T(8,128)(2,1)S(1)}, u32[]{:S(2)}, u32[]{:S(2)}) collective-permute-start(bf16[192,256]{1,0:T(8,128)(2,1)S(1)} %get-tuple-element.55.refs_0_), channel_id=1, source_target_pairs={{0,6},{2,4},{4,2},{6,0},{1,7},{3,5},{5,3},{7,1},{8,14},{10,12},{12... | collective-permute-start | bytes 294920 | tf_op jit(solution)/shard_map/ppermute | solution.py:23
  51.7 4.2 %copy-start.10 = (bf16[192,256]{1,0:T(8,128)(2,1)}, bf16[192,256]{1,0:T(8,128)(2,1)S(1)}, u32[]{:S(2)}) copy-start(bf16[192,256]{1,0:T(8,128)(2,1)S(1)} %collective-permute-done.8.refs_2_) | copy-start | bytes 294916
  56.0 16.1 %collective-permute-start.10 = (bf16[3072,256]{1,0:T(8,128)(2,1)S(1)}, bf16[3072,256]{1,0:T(8,128)(2,1)S(1)}, u32[]{:S(2)}, u32[]{:S(2)}) collective-permute-start(bf16[3072,256]{1,0:T(8,128)(2,1)S(1)} %shard_map.59), channel_id=1, source_target_pairs={{0,1},{1,0},{2,3},{3,2},{4,5},{5,4},{6,7},{7,6},{8,9},{9,8},{10,11... | collective-permute-start | bytes 4718600 | tf_op jit(solution)/shard_map/ppermute | solution.py:23
  60.4 17.7 %collective-permute-start.11 = (bf16[768,256]{1,0:T(8,128)(2,1)S(1)}, bf16[768,256]{1,0:T(8,128)(2,1)}, u32[]{:S(2)}, u32[]{:S(2)}) collective-permute-start(bf16[768,256]{1,0:T(8,128)(2,1)S(1)} %shard_map.63.refs_0_), channel_id=1, source_target_pairs={{0,8},{8,0},{16,24},{24,16},{1,9},{9,1},{17,25},{25,17},{2,10},{10... | collective-permute-start | bytes 1179656 | tf_op jit(solution)/shard_map/ppermute | solution.py:23
  60.5 23.0 %collective-permute-start.12 = (bf16[768,256]{1,0:T(8,128)(2,1)S(1)}, bf16[768,256]{1,0:T(8,128)(2,1)}, u32[]{:S(2)}, u32[]{:S(2)}) collective-permute-start(bf16[768,256]{1,0:T(8,128)(2,1)S(1)} %shard_map.63.refs_0_), channel_id=1, source_target_pairs={{0,16},{8,24},{16,0},{24,8},{1,17},{9,25},{17,1},{25,9},{2,18},{10... | collective-permute-start | bytes 1179656 | tf_op jit(solution)/shard_map/ppermute | solution.py:23
  65.3 20.7 %collective-permute-start.13 = (bf16[768,256]{1,0:T(8,128)(2,1)S(1)}, bf16[768,256]{1,0:T(8,128)(2,1)}, u32[]{:S(2)}, u32[]{:S(2)}) collective-permute-start(bf16[768,256]{1,0:T(8,128)(2,1)S(1)} %shard_map.63.refs_0_), channel_id=1, source_target_pairs={{0,24},{8,16},{16,8},{24,0},{1,25},{9,17},{17,9},{25,1},{2,26},{10... | collective-permute-start | bytes 1179656 | tf_op jit(solution)/shard_map/ppermute | solution.py:23
  66.1 2.3 %copy-start.3 = (bf16[3072,768]{1,0:T(8,128)(2,1)S(1)}, bf16[3072,768]{1,0:T(8,128)(2,1)}, u32[]{:S(2)}) copy-start(bf16[3072,768]{1,0:T(8,128)(2,1)} %all-gather.2.cloned.1.call-done.w) | copy-start | bytes 14155780
  70.1 34.8 %copy-start = (bf16[2,1536,768]{2,1,0:T(8,128)(2,1)}, bf16[2,1536,768]{2,1,0:T(8,128)(2,1)S(1)}, u32[]{:S(2)}) copy-start(bf16[2,1536,768]{2,1,0:T(8,128)(2,1)S(1)} %shard_map.60.w) | copy-start | bytes 14155780
  74.1 14.6 %copy-start.15 = (bf16[512,768]{1,0:T(8,128)(2,1)S(1)}, bf16[512,768]{1,0:T(8,128)(2,1)}, u32[]{:S(2)}) copy-start(bf16[512,768]{1,0:T(8,128)(2,1)} %param.5) | copy-start | bytes 2359300
  74.1 12.9 %collective-permute-start.14 = (bf16[256,768]{1,0:T(8,128)(2,1)S(1)}, bf16[256,768]{1,0:T(8,128)(2,1)S(1)}, u32[]{:S(2)}, u32[]{:S(2)}) collective-permute-start(bf16[256,768]{1,0:T(8,128)(2,1)S(1)} %get-tuple-element.59), channel_id=1, source_target_pairs={{0,128},{128,0},{1,129},{129,1},{2,130},{130,2},{3,131},{131,3},{4... | collective-permute-start | bytes 1179656 | tf_op jit(solution)/shard_map/ppermute | solution.py:23
  88.4 4.7 %collective-permute-start.15 = (bf16[3072,256]{1,0:T(8,128)(2,1)S(1)}, bf16[3072,256]{1,0:T(8,128)(2,1)S(1)}, u32[]{:S(2)}, u32[]{:S(2)}) collective-permute-start(bf16[3072,256]{1,0:T(8,128)(2,1)S(1)} %shard_map.64), channel_id=1, source_target_pairs={{0,1},{1,0},{2,3},{3,2},{4,5},{5,4},{6,7},{7,6},{8,9},{9,8},{10,11... | collective-permute-start | bytes 4718600 | tf_op jit(solution)/shard_map/ppermute | solution.py:23
  89.4 11.6 %collective-permute-start.16 = (bf16[256,768]{1,0:T(8,128)(2,1)S(1)}, bf16[256,768]{1,0:T(8,128)(2,1)S(1)}, u32[]{:S(2)}, u32[]{:S(2)}) collective-permute-start(bf16[256,768]{1,0:T(8,128)(2,1)S(1)} %get-tuple-element.96.g0.refs_0_), channel_id=1, source_target_pairs={{0,128},{128,0},{1,129},{129,1},{2,130},{130,2},{3,131},{131,3},{4... | collective-permute-start | bytes 1179656 | tf_op jit(solution)/shard_map/ppermute | solution.py:23
  103.0 4.0 %collective-permute-start.18 = (bf16[4,768,256]{2,1,0:T(8,128)(2,1)S(1)}, bf16[4,768,256]{2,1,0:T(8,128)(2,1)S(1)}, u32[]{:S(2)}, u32[]{:S(2)}) collective-permute-start(bf16[4,768,256]{2,1,0:T(8,128)(2,1)S(1)} %shard_map.68), channel_id=1, source_target_pairs={{0,1},{1,0},{2,3},{3,2},{4,5},{5,4},{6,7},{7,6},{8,9},{9,8},{10,11... | collective-permute-start | bytes 4718600 | tf_op jit(solution)/shard_map/ppermute | solution.py:23
  103.1 11.5 %collective-permute-start.17 = (bf16[256,768]{1,0:T(8,128)(2,1)S(1)}, bf16[256,768]{1,0:T(8,128)(2,1)S(1)}, u32[]{:S(2)}, u32[]{:S(2)}) collective-permute-start(bf16[256,768]{1,0:T(8,128)(2,1)S(1)} %get-tuple-element.67), channel_id=1, source_target_pairs={{0,128},{128,0},{1,129},{129,1},{2,130},{130,2},{3,131},{131,3},{4... | collective-permute-start | bytes 1179656 | tf_op jit(solution)/shard_map/ppermute | solution.py:23
  107.4 9.8 %copy-start.14 = (bf16[4,768,256]{2,1,0:T(8,128)(2,1)}, bf16[4,768,256]{2,1,0:T(8,128)(2,1)S(1)}, u32[]{:S(2)}) copy-start(bf16[4,768,256]{2,1,0:T(8,128)(2,1)S(1)} %add_convert_fusion.1) | copy-start | bytes 4718596
  115.3 24.9 %copy-start.5 = (bf16[3072,256]{1,0:T(8,128)(2,1)S(1)}, bf16[3072,256]{1,0:T(8,128)(2,1)}, u32[]{:S(2)}) copy-start(bf16[3072,256]{1,0:T(8,128)(2,1)} %copy-done.4) | copy-start | bytes 4718596
  115.3 10.7 %collective-permute-start.19 = (bf16[256,768]{1,0:T(8,128)(2,1)S(1)}, bf16[256,768]{1,0:T(8,128)(2,1)S(1)}, u32[]{:S(2)}, u32[]{:S(2)}) collective-permute-start(bf16[256,768]{1,0:T(8,128)(2,1)S(1)} %get-tuple-element.93.g0.refs_2_), channel_id=1, source_target_pairs={{0,128},{128,0},{1,129},{129,1},{2,130},{130,2},{3,131},{131,3},{4... | collective-permute-start | bytes 1179656 | tf_op jit(solution)/shard_map/ppermute | solution.py:23
  117.2 12.1 %collective-permute-start.20 = (bf16[768,256]{1,0:T(8,128)(2,1)S(1)}, bf16[768,256]{1,0:T(8,128)(2,1)S(1)}, u32[]{:S(2)}, u32[]{:S(2)}) collective-permute-start(bf16[768,256]{1,0:T(8,128)(2,1)S(1)} %get-tuple-element.92), channel_id=1, source_target_pairs={{0,8},{8,0},{16,24},{24,16},{1,9},{9,1},{17,25},{25,17},{2,10},{10... | collective-permute-start | bytes 1179656 | tf_op jit(solution)/shard_map/ppermute | solution.py:23
  117.3 20.2 %collective-permute-start.21 = (bf16[768,256]{1,0:T(8,128)(2,1)S(1)}, bf16[768,256]{1,0:T(8,128)(2,1)S(1)}, u32[]{:S(2)}, u32[]{:S(2)}) collective-permute-start(bf16[768,256]{1,0:T(8,128)(2,1)S(1)} %get-tuple-element.91), channel_id=1, source_target_pairs={{0,16},{8,24},{16,0},{24,8},{1,17},{9,25},{17,1},{25,9},{2,18},{10... | collective-permute-start | bytes 1179656 | tf_op jit(solution)/shard_map/ppermute | solution.py:23
  120.6 19.6 %collective-permute-start.22 = (bf16[768,256]{1,0:T(8,128)(2,1)S(1)}, bf16[768,256]{1,0:T(8,128)(2,1)}, u32[]{:S(2)}, u32[]{:S(2)}) collective-permute-start(bf16[768,256]{1,0:T(8,128)(2,1)S(1)} %get-tuple-element.90), channel_id=1, source_target_pairs={{0,24},{8,16},{16,8},{24,0},{1,25},{9,17},{17,9},{25,1},{2,26},{10... | collective-permute-start | bytes 1179656 | tf_op jit(solution)/shard_map/ppermute | solution.py:23
  129.3 10.9 %copy-start.16 = (bf16[768,256]{1,0:T(8,128)(2,1)}, bf16[768,256]{1,0:T(8,128)(2,1)S(1)}, u32[]{:S(2)}) copy-start(bf16[768,256]{1,0:T(8,128)(2,1)S(1)} %collective-permute-done.20) | copy-start | bytes 1179652
  137.5 2.7 %copy-start.18 = (bf16[768,256]{1,0:T(8,128)(2,1)}, bf16[768,256]{1,0:T(8,128)(2,1)S(1)}, u32[]{:S(2)}) copy-start(bf16[768,256]{1,0:T(8,128)(2,1)S(1)} %collective-permute-done.21) | copy-start | bytes 1179652
  148.5 2.3 %copy-start.1 = (bf16[2,1536,768]{2,1,0:T(8,128)(2,1)S(1)}, bf16[2,1536,768]{2,1,0:T(8,128)(2,1)}, u32[]{:S(2)}) copy-start(bf16[2,1536,768]{2,1,0:T(8,128)(2,1)} %copy-done) | copy-start | bytes 14155780
  152.9 3.5 %collective-permute-start.23 = (bf16[4,768,256]{2,1,0:T(8,128)(2,1)S(1)}, bf16[4,768,256]{2,1,0:T(8,128)(2,1)S(1)}, u32[]{:S(2)}, u32[]{:S(2)}) collective-permute-start(bf16[4,768,256]{2,1,0:T(8,128)(2,1)S(1)} %shard_map.70), channel_id=1, source_target_pairs={{0,1},{1,0},{2,3},{3,2},{4,5},{5,4},{6,7},{7,6},{8,9},{9,8},{10,11... | collective-permute-start | bytes 4718600 | tf_op jit(solution)/shard_map/ppermute | solution.py:23
  156.8 20.8 %collective-permute-start.24 = (bf16[768,256]{1,0:T(8,128)(2,1)S(1)}, bf16[768,256]{1,0:T(8,128)(2,1)S(1)}, u32[]{:S(2)}, u32[]{:S(2)}) collective-permute-start(bf16[768,256]{1,0:T(8,128)(2,1)S(1)} %get-tuple-element.89), channel_id=1, source_target_pairs={{0,8},{8,0},{16,24},{24,16},{1,9},{9,1},{17,25},{25,17},{2,10},{10... | collective-permute-start | bytes 1179656 | tf_op jit(solution)/shard_map/ppermute | solution.py:23
  156.9 20.8 %collective-permute-start.25 = (bf16[768,256]{1,0:T(8,128)(2,1)S(1)}, bf16[768,256]{1,0:T(8,128)(2,1)S(1)}, u32[]{:S(2)}, u32[]{:S(2)}) collective-permute-start(bf16[768,256]{1,0:T(8,128)(2,1)S(1)} %get-tuple-element.88), channel_id=1, source_target_pairs={{0,16},{8,24},{16,0},{24,8},{1,17},{9,25},{17,1},{25,9},{2,18},{10... | collective-permute-start | bytes 1179656 | tf_op jit(solution)/shard_map/ppermute | solution.py:23
  159.7 20.6 %collective-permute-start.26 = (bf16[768,256]{1,0:T(8,128)(2,1)S(1)}, bf16[768,256]{1,0:T(8,128)(2,1)S(1)}, u32[]{:S(2)}, u32[]{:S(2)}) collective-permute-start(bf16[768,256]{1,0:T(8,128)(2,1)S(1)} %get-tuple-element.87), channel_id=1, source_target_pairs={{0,24},{8,16},{16,8},{24,0},{1,25},{9,17},{17,9},{25,1},{2,26},{10... | collective-permute-start | bytes 1179656 | tf_op jit(solution)/shard_map/ppermute | solution.py:23
  161.7 5.6 %collective-permute-start.27 = (bf16[192,256]{1,0:T(8,128)(2,1)S(1)}, bf16[192,256]{1,0:T(8,128)(2,1)S(1)}, u32[]{:S(2)}, u32[]{:S(2)}) collective-permute-start(bf16[192,256]{1,0:T(8,128)(2,1)S(1)} %get-tuple-element.102), channel_id=1, source_target_pairs={{0,2},{2,0},{4,6},{6,4},{1,3},{3,1},{5,7},{7,5},{8,10},{10,8},{12,... | collective-permute-start | bytes 294920 | tf_op jit(solution)/shard_map/ppermute | solution.py:23
  161.9 11.1 %collective-permute-start.28 = (bf16[192,256]{1,0:T(8,128)(2,1)S(1)}, bf16[192,256]{1,0:T(8,128)(2,1)S(1)}, u32[]{:S(2)}, u32[]{:S(2)}) collective-permute-start(bf16[192,256]{1,0:T(8,128)(2,1)S(1)} %get-tuple-element.101), channel_id=1, source_target_pairs={{0,4},{2,6},{4,0},{6,2},{1,5},{3,7},{5,1},{7,3},{8,12},{10,14},{12... | collective-permute-start | bytes 294920 | tf_op jit(solution)/shard_map/ppermute | solution.py:23
  167.3 10.4 %collective-permute-start.29 = (bf16[192,256]{1,0:T(8,128)(2,1)S(1)}, bf16[192,256]{1,0:T(8,128)(2,1)S(1)}, u32[]{:S(2)}, u32[]{:S(2)}) collective-permute-start(bf16[192,256]{1,0:T(8,128)(2,1)S(1)} %get-tuple-element.100), channel_id=1, source_target_pairs={{0,6},{2,4},{4,2},{6,0},{1,7},{3,5},{5,3},{7,1},{8,14},{10,12},{12... | collective-permute-start | bytes 294920 | tf_op jit(solution)/shard_map/ppermute | solution.py:23
  180.6 10.2 %collective-permute-start.30 = (bf16[192,256]{1,0:T(8,128)(2,1)S(1)}, bf16[192,256]{1,0:T(8,128)(2,1)S(1)}, u32[]{:S(2)}, u32[]{:S(2)}) collective-permute-start(bf16[192,256]{1,0:T(8,128)(2,1)S(1)} %get-tuple-element.99), channel_id=1, source_target_pairs={{0,2},{2,0},{4,6},{6,4},{1,3},{3,1},{5,7},{7,5},{8,10},{10,8},{12,... | collective-permute-start | bytes 294920 | tf_op jit(solution)/shard_map/ppermute | solution.py:23
  180.7 10.1 %collective-permute-start.31 = (bf16[192,256]{1,0:T(8,128)(2,1)S(1)}, bf16[192,256]{1,0:T(8,128)(2,1)S(1)}, u32[]{:S(2)}, u32[]{:S(2)}) collective-permute-start(bf16[192,256]{1,0:T(8,128)(2,1)S(1)} %get-tuple-element.98), channel_id=1, source_target_pairs={{0,4},{2,6},{4,0},{6,2},{1,5},{3,7},{5,1},{7,3},{8,12},{10,14},{12... | collective-permute-start | bytes 294920 | tf_op jit(solution)/shard_map/ppermute | solution.py:23
  184.7 10.2 %collective-permute-start.32 = (bf16[192,256]{1,0:T(8,128)(2,1)S(1)}, bf16[192,256]{1,0:T(8,128)(2,1)S(1)}, u32[]{:S(2)}, u32[]{:S(2)}) collective-permute-start(bf16[192,256]{1,0:T(8,128)(2,1)S(1)} %get-tuple-element.97), channel_id=1, source_target_pairs={{0,6},{2,4},{4,2},{6,0},{1,7},{3,5},{5,3},{7,1},{8,14},{10,12},{12... | collective-permute-start | bytes 294920 | tf_op jit(solution)/shard_map/ppermute | solution.py:23
  187.2 9.8 %collective-permute-start.33 = (bf16[192,256]{1,0:T(8,128)(2,1)S(1)}, bf16[192,256]{1,0:T(8,128)(2,1)S(1)}, u32[]{:S(2)}, u32[]{:S(2)}) collective-permute-start(bf16[192,256]{1,0:T(8,128)(2,1)S(1)} %fusion.22), channel_id=1, source_target_pairs={{0,0},{8,8},{136,16},{128,24},{24,128},{16,136},{144,144},{152,152... | collective-permute-start | bytes 294920 | tf_op jit(solution)/shard_map/ppermute | solution.py:44
  197.0 8.6 %collective-permute-start.34 = (bf16[192,256]{1,0:T(8,128)(2,1)S(1)}, bf16[192,256]{1,0:T(8,128)(2,1)S(1)}, u32[]{:S(2)}, u32[]{:S(2)}) collective-permute-start(bf16[192,256]{1,0:T(8,128)(2,1)S(1)} %add_convert_fusion.2), channel_id=1, source_target_pairs={{0,0},{8,8},{136,16},{128,24},{24,128},{16,136},{144,144},{152,152... | collective-permute-start | bytes 294920 | tf_op jit(solution)/shard_map/ppermute | solution.py:44
  (9 other events, 13.9 us)
Sparse Core Ops, SparseCore 0:
  9.8 56.2 all-gather.1
  148.6 49.0 reduce-scatter.1

commit v2 on v1

v2 whole, which is shorter than its diff:
```python
import functools
import math

import jax
import jax.numpy as jnp
from jax import lax
from jax.experimental import pallas as pl
from jax.experimental.pallas import tpu as pltpu
from jax.sharding import Mesh
from jax.sharding import PartitionSpec as P

slope_coef = math.sqrt(2.0 / math.pi)
AXES = ("zl", "x", "y", "zh", "c")
SIZES = {"zl": 2, "x": 4, "y": 4, "zh": 4, "c": 2}
BF16, F32 = jnp.bfloat16, jnp.float32
MIB = 1024 * 1024
HBM = pl.BlockSpec(memory_space=pl.ANY)
VMEM = pl.BlockSpec(memory_space=pltpu.VMEM)
SMEM = pl.BlockSpec(memory_space=pltpu.SMEM)


def flip(value, axis, mask):
    return lax.ppermute(value, axis, [(i, i ^ mask) for i in range(SIZES[axis])])


def over_z(value):
    return flip(value, "zl", 1)


def over_near(value):
    return flip(value, "y", 1)


def over_far(value):
    return flip(value, "y", 3)


def add_top(block, came):
    n = came.shape[0]
    return jnp.concatenate([added(block[:n], [came]).astype(BF16), block[n:]])


def add_low(block, came):
    n = block.shape[0] - came.shape[0]
    return jnp.concatenate([block[:n], added(block[n:], [came]).astype(BF16)])


def spread_pairs(turn):
    pairs = []
    for zl in range(2):
        for y in range(4):
            to_y = y if y >> 1 == zl ^ turn else y ^ 3
            pairs.append((zl * 4 + y, (y >> 1) * 4 + to_y))
    return pairs


def spread(value, turn):
    return lax.ppermute(value, ("zl", "y"), spread_pairs(turn))


def spread_back(value, turn):
    return lax.ppermute(value, ("zl", "y"), [(b, a) for a, b in spread_pairs(turn)])


def call(kernel, out_shape, in_specs, out_specs, scratch, flops, nbytes, limit):
    return pl.pallas_call(
        kernel,
        out_shape=out_shape,
        in_specs=in_specs,
        out_specs=out_specs,
        scratch_shapes=scratch,
        compiler_params=pltpu.CompilerParams(vmem_limit_bytes=limit),
        cost_estimate=pl.CostEstimate(flops=flops, bytes_accessed=nbytes, transcendentals=0),
    )


def run_copies(copies):
    for copy in copies:
        copy.start()
    for copy in copies:
        copy.wait()


def weight_row(idx, near, dz, dc):
    zl, y, zh, c = idx[0], idx[2], idx[3], idx[4]
    upper = near ^ zl ^ (y & 1) ^ (y >> 1)
    return pl.multiple_of(((upper * 4 + (zh ^ dz)) * 2 + (c ^ dc)) * 192, 192)


def join_kernel(n, *refs):
    *ins, out, sems = refs
    copies = []
    for i, a in enumerate(ins):
        copies.append(pltpu.make_async_copy(a, out.at[pl.ds(i * n, n), :], sems.at[i]))
    run_copies(copies)


def join(*values):
    rows, width = values[0].shape
    return call(
        functools.partial(join_kernel, rows),
        jax.ShapeDtypeStruct((len(values) * rows, width), BF16),
        [HBM] * len(values),
        VMEM,
        [pltpu.SemaphoreType.DMA((len(values),))],
        0,
        4 * len(values) * rows * width,
        8 * MIB,
    )(*values)


def across(a, w):
    return lax.dot_general(a, w, (((0,), (0,)), ((), ())), preferred_element_type=F32)


def turn_of(idx):
    return idx[2] >> 1


def project_kernel(idx, own, other, w, out, w0, w1, a_v, w_v, acc, a_sems, w_sems, out_sems):
    loads = [
        pltpu.make_async_copy(a, a_v.at[dc], a_sems.at[dc]) for dc, a in enumerate((own, other))
    ]
    copies = []
    for dc in range(2):
        for near in range(2):
            for dz in range(4):
                copies.append(
                    pltpu.make_async_copy(
                        w.at[pl.ds(weight_row(idx, near, dz, dc), 192), :],
                        w_v.at[dc, pl.ds((near * 4 + dz) * 192, 192), :],
                        w_sems.at[len(copies)],
                    )
                )
    loads[0].start()
    for copy in copies[:8]:
        copy.start()
    loads[1].start()
    for copy in copies[8:]:
        copy.start()
    stores = []
    n = a_v.shape[-1]
    for step in range(4):
        dc, near = step // 2, step % 2
        if near == 0:
            loads[dc].wait()
        for copy in copies[4 * step : 4 * step + 4]:
            copy.wait()
        if near == 1:
            stores.append(pltpu.make_async_copy(w_v.at[dc], (w0, w1)[dc], out_sems.at[dc]))
            stores[-1].start()
        rows = slice(near * 768, near * 768 + 768)
        for half in range(2):
            part = across(a_v[dc, half ^ turn_of(idx), rows], w_v[dc, rows])
            if step > 0:
                part = acc[half] + part
            if step < 3:
                acc[half] = part
            else:
                out[half * n : half * n + n] = part.astype(BF16)
    for store in stores:
        store.wait()


def project(idx, own, other, w_all):
    width = own.shape[-1]
    return call(
        project_kernel,
        [jax.ShapeDtypeStruct((2 * width, 768), BF16)]
        + [jax.ShapeDtypeStruct((1536, 768), BF16)] * 2,
        [SMEM, HBM, HBM, HBM],
        [VMEM, HBM, HBM],
        [
            pltpu.VMEM((2, 2, 1536, width), BF16),
            pltpu.VMEM((2, 1536, 768), BF16),
            pltpu.VMEM((2, width, 768), F32),
            pltpu.SemaphoreType.DMA((2,)),
            pltpu.SemaphoreType.DMA((16,)),
            pltpu.SemaphoreType.DMA((2,)),
        ],
        16 * width * 768 * 768,
        20 << 20,
        58 * MIB,
    )(idx, own.reshape(2, 1536, width), other.reshape(2, 1536, width), w_all)


def half_kernel(idx, a, w, *refs):
    *acc, out = refs
    n = a.shape[-1]
    for half in range(2):
        rows = slice(half * n, half * n + n)
        part = across(a[half ^ turn_of(idx)], w[...])
        out[rows] = acc[0][rows] + part if acc else part


def project_half(idx, a, w, acc):
    width = a.shape[-1]
    return call(
        half_kernel,
        jax.ShapeDtypeStruct((2 * width, 768), F32),
        [SMEM] + [VMEM] * (2 + len(acc)),
        VMEM,
        [],
        8 * width * 768 * 768,
        20 * 1024 * width,
        20 * MIB,
    )(idx, a.reshape(2, 1536, width), w, *acc)


def input_grad_kernel(idx, g, w, out):
    n = out.shape[-1]
    for half in range(2):
        upper = half ^ turn_of(idx)
        part = lax.dot_general(
            w[...],
            g[half * n : half * n + n],
            (((1,), (1,)), ((), ())),
            preferred_element_type=F32,
        ).astype(BF16)
        for near in range(2):
            out[upper * 2 + (near ^ upper)] = part[near * 768 : near * 768 + 768]


def input_grad(idx, g, w):
    width = g.shape[0] // 2
    return call(
        input_grad_kernel,
        jax.ShapeDtypeStruct((4, 768, width), BF16),
        [SMEM] + [VMEM] * 2,
        VMEM,
        [],
        8 * width * 768 * 768,
        20 * 1024 * width,
        20 * MIB,
    )(idx, g, w)


def weight_grad_kernel(idx, g, own, other, *refs):
    *acc, out = refs
    n = own.shape[-1]
    for dc, a in enumerate((own, other)):
        for near in range(2):
            total = None
            for half in range(2):
                term = jnp.dot(
                    a[half ^ turn_of(idx), near * 768 : near * 768 + 768, :],
                    g[half * n : half * n + n],
                    preferred_element_type=F32,
                )
                total = term if total is None else total + term
            for dz in range(4):
                part = total[dz * 192 : dz * 192 + 192]
                rows = pl.ds(weight_row(idx, near, dz, dc), 192)
                if acc:
                    part = part + acc[0][rows, :].astype(F32)
                out[rows, :] = part.astype(BF16)


def weight_grad(idx, g, own, other, acc):
    width = own.shape[-1]
    return call(
        weight_grad_kernel,
        jax.ShapeDtypeStruct((3072, 768), BF16),
        [SMEM] + [VMEM] * (3 + len(acc)),
        VMEM,
        [],
        16 * width * 768 * 768,
        16 << 20,
        24 * MIB,
    )(idx, g, own.reshape(2, 1536, width), other.reshape(2, 1536, width), *acc)


def gelu_pair(pre_act, grad_out):
    inside = slope_coef * (pre_act + 0.044715 * pre_act * pre_act * pre_act)
    tangent = jnp.tanh(inside)
    activated = 0.5 * pre_act * (1.0 + tangent)
    slope = 0.5 * (1.0 + tangent) + 0.5 * pre_act * (1.0 - tangent * tangent) * slope_coef * (
        1.0 + 3.0 * 0.044715 * pre_act * pre_act
    )
    return activated.astype(BF16), (grad_out.astype(F32) * slope).astype(BF16)


def stage(*values):
    return lax.optimization_barrier(values)


def added(first, others):
    total = first.astype(F32)
    for other in others:
        total = total + other.astype(F32)
    return total


def gather_pieces(value, axis):
    return [value] + [flip(value, axis, d) for d in (1, 2, 3)]


def in_order(planes):
    return join(planes[0], planes[1], planes[3], planes[2])


def per_device(tokens, weight, grad_out):
    idx = jnp.stack([lax.axis_index(axis) for axis in AXES]).astype(jnp.int32)
    n = 256
    w_all = lax.all_gather(weight, "x", axis=0, tiled=True)
    zl, upper = idx[0], idx[2] >> 1
    turned = tokens.T
    first, last = turned[:, :n], turned[:, n:]
    came0 = spread(jnp.where(zl == 0, first, last), 0)
    came1 = spread(jnp.where(zl == 0, last, first), 1)
    piece_p = jnp.where(upper == zl, came1, came0)
    piece_o = jnp.where(upper == zl, came0, came1)
    *pieces_p, piece_o = stage(*gather_pieces(piece_p, "zh"), piece_o)

    pieces_o = gather_pieces(piece_o, "zh")
    planes_p = gather_pieces(join(*pieces_p), "y")
    stages = stage(*planes_p, *pieces_o)
    planes_p, pieces_o = stages[:4], stages[4:]

    own_p = in_order(planes_p)
    planes_o = gather_pieces(join(*pieces_o), "y")
    other_p = flip(own_p, "c", 1)
    send, w0, w1 = project(idx, own_p, other_p, w_all)
    came = over_z(send)
    *planes_o, w0 = stage(*planes_o, w0)

    own_o = in_order(planes_o)
    other_o = flip(own_o, "c", 1)
    pre_act = project_half(idx, other_o, w1, [project_half(idx, own_o, w0, [])])
    activated, grad_o = gelu_pair(added(pre_act, [came]), grad_out)
    grad_p = over_z(grad_o)

    half = flip(input_grad(idx, grad_o, w1), "c", 1)
    both_o = added(input_grad(idx, grad_o, w0), [half]).astype(BF16)
    rows_o = [flip(both_o[d], "y", d) for d in (1, 2, 3)]
    partial = weight_grad(idx, grad_o, own_o, other_o, [])
    grad_p, partial, *rows_o = stage(grad_p, partial, *rows_o)

    partial = weight_grad(idx, grad_p, own_p, other_p, [partial])
    partial, grad_p = stage(partial, grad_p)
    grad_weight = lax.psum_scatter(partial, "x", scatter_dimension=0, tiled=True)
    half = flip(input_grad(idx, grad_p, w1), "c", 1)
    both_p = added(input_grad(idx, grad_p, w0), [half]).astype(BF16)
    rows_p = [flip(both_p[d], "y", d) for d in (1, 2, 3)]
    line_o = added(both_o[0], rows_o).astype(BF16).reshape(4, 192, n)
    homes_o = [flip(line_o[d], "zh", d) for d in (1, 2, 3)]
    stages = stage(*rows_p, *homes_o)
    rows_p, homes_o = stages[:3], stages[3:]
    line_p = added(both_p[0], rows_p).astype(BF16).reshape(4, 192, n)
    homes_p = [flip(line_p[d], "zh", d) for d in (1, 2, 3)]
    final_o = added(line_o[0], homes_o).astype(BF16)
    final_p = added(line_p[0], homes_p).astype(BF16)
    back0 = spread_back(jnp.where(upper == zl, final_o, final_p), 0)
    back1 = spread_back(jnp.where(upper == zl, final_p, final_o), 1)
    first = jnp.where(zl == 0, back0, back1)
    last = jnp.where(zl == 0, back1, back0)
    grad_tokens = jnp.concatenate([first, last], axis=1).T
    return activated, grad_tokens, grad_weight


def solution(mesh):
    fine = Mesh(mesh.devices.reshape(2, 4, 4, 4, 2), AXES)
    spec = P(("zl", "x"), ("y", "zh", "c"))
    return jax.shard_map(
        per_device, mesh=fine, in_specs=(spec,) * 3, out_specs=(spec,) * 3, check_vma=False
    )
```

time: 214 us -> 200 us (0.935)
  starting transfers between devices: 76.3 us -> 63 us
  local copies, waits for them, and re-layouts: 10.8 us -> 4.54 us
  Pallas kernels: 27 us -> 30.2 us
    ppermute x32 -> x30, starting transfers between devices: 65.6 us -> 54.5 us  [flip(): lax.ppermute(value, axis, [(i, i ^ mask) for i in range(SIZES[axis])])]
    unnamed x40 -> x32, local copies, waits for them, and re-layouts: 10.5 us -> 3.72 us
    all_gather x1, waiting for transfers between devices: 0.73 us -> 4.74 us  [per_device(): w_all = lax.all_gather(weight, 'x', axis=0, tiled=True)]
    pallas_call x10 -> x9, Pallas kernels: 23.7 us -> 26.7 us  [the longest x4 8.12 us: input_grad(): call(input_grad_kernel, jax.ShapeDtypeStruct((4, 768, width), BF16), [SME...]
    ppermute x3 -> x4, waiting for transfers between devices: 13.6 us -> 11.1 us  [the longest x2 6.33 us: spread(): return lax.ppermute(value, ('zl', 'y'), spread_pairs(turn))]
    ppermute x3 -> x4, starting transfers between devices: 10.6 us -> 8.47 us  [the longest x2 4.55 us: spread(): return lax.ppermute(value, ('zl', 'y'), spread_pairs(turn))]
    ppermute x32 -> x30, waiting for transfers between devices: 64.4 us -> 64.9 us  [flip(): lax.ppermute(value, axis, [(i, i ^ mask) for i in range(SIZES[axis])])]
  transfers between devices with their start and end apart: 37 -> 36, of which waited for: 25 -> 22; matrix products, arithmetic and copies ran while one was open for 2% -> 2% of each run, Pallas kernels for 8% -> 12%
where the time goes in v2:
time: 200 us
  waiting for transfers between devices  81.4 us (41%)
  starting transfers between devices  63 us (32%)
  Pallas kernels  30.2 us (15%)
  between operations  14.5 us (7%)
  other arithmetic  6.14 us (3%)
  local copies, waits for them, and re-layouts  4.54 us (2%)
    ppermute x30, waiting for transfers between devices, flip(): lax.ppermute(value, axis, [(i, i ^ mask) for i in range(SIZES[axis])])  64.9 us
    ppermute x30, starting transfers between devices, flip(): lax.ppermute(value, axis, [(i, i ^ mask) for i in range(SIZES[axis])])  54.5 us
    pallas_call x4, Pallas kernels, input_grad(): call(input_grad_kernel, jax.ShapeDtypeStruct((4, 768, width), BF16), [SME...  8.12 us
    pallas_call x1, Pallas kernels, project(): call(project_kernel, [jax.ShapeDtypeStruct((2 * width, 768), BF16)] + [ja...  7.99 us
    pallas_call x2, Pallas kernels, weight_grad(): call(weight_grad_kernel, jax.ShapeDtypeStruct((3072, 768), BF16), [SMEM]...  6.68 us
    ppermute x2, waiting for transfers between devices, spread(): return lax.ppermute(value, ('zl', 'y'), spread_pairs(turn))  6.33 us
    ppermute x2, waiting for transfers between devices, spread_back(): lax.ppermute(value, ('zl', 'y'), [(b, a) for a, b in spread_pairs(turn)])  4.77 us
    all_gather x1, waiting for transfers between devices, per_device(): w_all = lax.all_gather(weight, 'x', axis=0, tiled=True)  4.74 us
  transfers between devices with their start and end apart: 36, of which 22 were waited for; matrix products, arithmetic and copies ran while one was open for 2% of the time, Pallas kernels for 12%

profile of v2, /device:TPU:38, one launch (start us, length us, event | category | flops | bytes accessed | tf_op | source)
XLA Modules:
  0.0 199.8 jit_solution(5693947591063837012)
XLA Ops:
  8.9 4.5 %collective-permute-start.1 = (bf16[192,256]{1,0:T(8,128)(2,1)S(1)}, bf16[192,256]{1,0:T(8,128)(2,1)S(1)}, u32[]{:S(2)}, u32[]{:S(2)}) collective-permute-start(bf16[192,256]{1,0:T(8,128)(2,1)S(1)} %get-tuple-element.92), channel_id=1, source_target_pairs={{0,0},{8,8},{16,136},{24,128},{128,24},{136,16},{144,144},{152,152... | collective-permute-start | bytes 294920 | tf_op jit(solution)/shard_map/ppermute | solution.py:58
  13.5 5.1 %collective-permute-done.1 = bf16[192,256]{1,0:T(8,128)(2,1)S(1)} collective-permute-done((bf16[192,256]{1,0:T(8,128)(2,1)S(1)}, bf16[192,256]{1,0:T(8,128)(2,1)S(1)}, u32[]{:S(2)}, u32[]{:S(2)}) %collective-permute-start.1) | collective-permute-done | bytes 98336 | tf_op jit(solution)/shard_map/ppermute | solution.py:58
  19.8 5.9 %collective-permute-start.4 = (bf16[192,256]{1,0:T(8,128)(2,1)S(1)}, bf16[192,256]{1,0:T(8,128)(2,1)S(1)}, u32[]{:S(2)}, u32[]{:S(2)}) collective-permute-start(bf16[192,256]{1,0:T(8,128)(2,1)S(1)} %get-tuple-element.37.refs_0_), channel_id=1, source_target_pairs={{0,6},{2,4},{4,2},{6,0},{1,7},{3,5},{5,3},{7,1},{8,14},{10,12},{12... | collective-permute-start | bytes 294920 | tf_op jit(solution)/shard_map/ppermute | solution.py:23
  26.8 1.5 collective-permute-start.2
  28.2 2.5 %collective-permute-done.4.refs_3_ = bf16[192,256]{1,0:T(8,128)(2,1)S(1)} collective-permute-done((bf16[192,256]{1,0:T(8,128)(2,1)S(1)}, bf16[192,256]{1,0:T(8,128)(2,1)S(1)}, u32[]{:S(2)}, u32[]{:S(2)}) %collective-permute-start.4) | collective-permute-done | bytes 98336 | tf_op jit(solution)/shard_map/ppermute | solution.py:23
  30.7 6.0 %collective-permute-done.3.refs_2_ = bf16[192,256]{1,0:T(8,128)(2,1)S(1)} collective-permute-done((bf16[192,256]{1,0:T(8,128)(2,1)S(1)}, bf16[192,256]{1,0:T(8,128)(2,1)S(1)}, u32[]{:S(2)}, u32[]{:S(2)}) %collective-permute-start.3) | collective-permute-done | bytes 98336 | tf_op jit(solution)/shard_map/ppermute | solution.py:23
  38.5 3.0 %collective-permute-start.5 = (bf16[768,256]{1,0:T(8,128)(2,1)S(1)}, bf16[768,256]{1,0:T(8,128)(2,1)S(1)}, u32[]{:S(2)}, u32[]{:S(2)}) collective-permute-start(bf16[768,256]{1,0:T(8,128)(2,1)S(1)} %shard_map.58.refs_0_), channel_id=1, source_target_pairs={{0,8},{8,0},{16,24},{24,16},{1,9},{9,1},{17,25},{25,17},{2,10},{10... | collective-permute-start | bytes 1179656 | tf_op jit(solution)/shard_map/ppermute | solution.py:23
  41.4 3.1 %collective-permute-start.10 = (bf16[192,256]{1,0:T(8,128)(2,1)S(1)}, bf16[192,256]{1,0:T(8,128)(2,1)S(1)}, u32[]{:S(2)}, u32[]{:S(2)}) collective-permute-start(bf16[192,256]{1,0:T(8,128)(2,1)S(1)} %get-tuple-element.42.refs_0_), channel_id=1, source_target_pairs={{0,6},{2,4},{4,2},{6,0},{1,7},{3,5},{5,3},{7,1},{8,14},{10,12},{12... | collective-permute-start | bytes 294920 | tf_op jit(solution)/shard_map/ppermute | solution.py:23
  44.5 2.1 %collective-permute-start.9 = (bf16[192,256]{1,0:T(8,128)(2,1)S(1)}, bf16[192,256]{1,0:T(8,128)(2,1)S(1)}, u32[]{:S(2)}, u32[]{:S(2)}) collective-permute-start(bf16[192,256]{1,0:T(8,128)(2,1)S(1)} %get-tuple-element.42.refs_0_), channel_id=1, source_target_pairs={{0,4},{2,6},{4,0},{6,2},{1,5},{3,7},{5,1},{7,3},{8,12},{10,14},{12... | collective-permute-start | bytes 294920 | tf_op jit(solution)/shard_map/ppermute | solution.py:23
  46.6 1.6 collective-permute-done.10.refs_3_
  48.2 1.6 collective-permute-start.8
  49.8 4.3 %collective-permute-done.9.refs_2_ = bf16[192,256]{1,0:T(8,128)(2,1)S(1)} collective-permute-done((bf16[192,256]{1,0:T(8,128)(2,1)S(1)}, bf16[192,256]{1,0:T(8,128)(2,1)S(1)}, u32[]{:S(2)}, u32[]{:S(2)}) %collective-permute-start.9) | collective-permute-done | bytes 98336 | tf_op jit(solution)/shard_map/ppermute | solution.py:23
  56.5 2.7 %collective-permute-start.13 = (bf16[768,256]{1,0:T(8,128)(2,1)S(1)}, bf16[768,256]{1,0:T(8,128)(2,1)}, u32[]{:S(2)}, u32[]{:S(2)}) collective-permute-start(bf16[768,256]{1,0:T(8,128)(2,1)S(1)} %shard_map.59.refs_0_), channel_id=1, source_target_pairs={{0,24},{8,16},{16,8},{24,0},{1,25},{9,17},{17,9},{25,1},{2,26},{10... | collective-permute-start | bytes 1179656 | tf_op jit(solution)/shard_map/ppermute | solution.py:23
  61.3 4.7 %all-gather.2.cloned.1.call-done.w = bf16[3072,768]{1,0:T(8,128)(2,1)} async-done(((bf16[768,768]{1,0:T(8,128)(2,1)}), bf16[3072,768]{1,0:T(8,128)(2,1)}) %all-gather.2.cloned.1.call-update) | async-done | bytes 4718608 | tf_op jit(solution)/shard_map/all_gather | solution.py:305
  66.1 8.0 %shard_map.61 = (bf16[512,768]{1,0:T(8,128)(2,1)}, bf16[1536,768]{1,0:T(8,128)(2,1)}, bf16[1536,768]{1,0:T(8,128)(2,1)}) custom-call(s32[5]{0:T(128)} %stack.23.idx, bf16[2,1536,256]{2,1,0:T(8,128)(2,1)} %bitcast.36, bf16[2,1536,256]{2,1,0:T(8,128)(2,1)} %bitcast.40, bf16[3072,768]{1,0:T(8,128)(2,1)} %all-gather.2.cloned.1.call-done.w), custom_call_target="tpu_custom_call" | custom-call | flops 2415919104 | bytes 20971520 | tf_op jit(solution)/shard_map/pallas_call | solution.py:167
  74.1 3.8 %collective-permute-done.13.refs_2_ = bf16[768,256]{1,0:T(8,128)(2,1)} collective-permute-done((bf16[768,256]{1,0:T(8,128)(2,1)S(1)}, bf16[768,256]{1,0:T(8,128)(2,1)}, u32[]{:S(2)}, u32[]{:S(2)}) %collective-permute-start.13) | collective-permute-done | bytes 393248 | tf_op jit(solution)/shard_map/ppermute | solution.py:23
  78.4 1.6 shard_map.62
  80.2 3.7 %collective-permute-start.16 = (bf16[512,768]{1,0:T(8,128)(2,1)S(1)}, bf16[512,768]{1,0:T(8,128)(2,1)S(1)}, u32[]{:S(2)}, u32[]{:S(2)}) collective-permute-start(bf16[512,768]{1,0:T(8,128)(2,1)S(1)} %copy-done.15), channel_id=1, source_target_pairs={{0,128},{128,0},{1,129},{129,1},{2,130},{130,2},{3,131},{131,3},{4... | collective-permute-start | bytes 2359304 | tf_op jit(solution)/shard_map/ppermute | solution.py:23
  83.9 2.0 shard_map.63.refs_0_
  85.9 2.0 shard_map.64
  87.9 13.9 %collective-permute-done.16 = bf16[512,768]{1,0:T(8,128)(2,1)S(1)} collective-permute-done((bf16[512,768]{1,0:T(8,128)(2,1)S(1)}, bf16[512,768]{1,0:T(8,128)(2,1)S(1)}, u32[]{:S(2)}, u32[]{:S(2)}) %collective-permute-start.16) | collective-permute-done | bytes 786464 | tf_op jit(solution)/shard_map/ppermute | solution.py:23
  101.8 2.1 %fusion.6 = (bf16[512,768]{1,0:T(8,128)(2,1)S(1)}, bf16[512,768]{1,0:T(8,128)(2,1)}) fusion(bf16[512,768]{1,0:T(8,128)(2,1)S(1)} %copy-done.10, f32[512,768]{1,0:T(8,128)S(1)} %shard_map.64, bf16[512,768]{1,0:T(8,128)(2,1)S(1)} %collective-permute-done.16), kind=kLoop, calls=%fused_computation.10 | loop fusion | flops 9437184 | bytes 4718592 | tf_op jit(solution)/shard_map/convert_element_type | solution.py:280
  103.9 2.0 %shard_map.66 = bf16[4,768,256]{2,1,0:T(8,128)(2,1)S(1)} custom-call(s32[5]{0:T(128)S(1)} %copy-done.8, bf16[512,768]{1,0:T(8,128)(2,1)S(1)} %get-tuple-element.74.g, bf16[1536,768]{1,0:T(8,128)(2,1)S(1)} %copy-done), custom_call_target="tpu_custom_call" | custom-call | flops 1207959552 | bytes 5242880 | tf_op jit(solution)/shard_map/pallas_call | solution.py:226
  106.1 1.8 collective-permute-start.18
  107.9 2.0 %shard_map.65 = bf16[4,768,256]{2,1,0:T(8,128)(2,1)S(1)} custom-call(s32[5]{0:T(128)S(1)} %copy-done.8, bf16[512,768]{1,0:T(8,128)(2,1)S(1)} %get-tuple-element.74.g, bf16[1536,768]{1,0:T(8,128)(2,1)S(1)} %copy-done.1), custom_call_target="tpu_custom_call" | custom-call | flops 1207959552 | bytes 5242880 | tf_op jit(solution)/shard_map/pallas_call | solution.py:226
  110.4 1.3 collective-permute-start.21
  112.7 1.9 collective-permute-start.19
  114.6 3.3 %shard_map.67.refs_0_ = bf16[3072,768]{1,0:T(8,128)(2,1)S(1)} custom-call(s32[5]{0:T(128)S(1)} %copy-done.8, bf16[512,768]{1,0:T(8,128)(2,1)S(1)} %get-tuple-element.74.g, bf16[2,1536,256]{2,1,0:T(8,128)(2,1)S(1)} %bitcast.35, bf16[2,1536,256]{2,1,0:T(8,128)(2,1)S(1)} %bitcast.39), custom_call_target="tpu_custom_call" | custom-call | flops 2415919104 | bytes 16777216 | tf_op jit(solution)/shard_map/pallas_call | solution.py:261
  117.9 8.1 %collective-permute-done.18.g = bf16[512,768]{1,0:T(8,128)(2,1)S(1)} collective-permute-done((bf16[512,768]{1,0:T(8,128)(2,1)S(1)}, bf16[512,768]{1,0:T(8,128)(2,1)S(1)}, u32[]{:S(2)}, u32[]{:S(2)}) %collective-permute-start.18) | collective-permute-done | bytes 786464 | tf_op jit(solution)/shard_map/ppermute | solution.py:23
  126.0 5.3 %collective-permute-done.21 = bf16[768,256]{1,0:T(8,128)(2,1)S(1)} collective-permute-done((bf16[768,256]{1,0:T(8,128)(2,1)S(1)}, bf16[768,256]{1,0:T(8,128)(2,1)S(1)}, u32[]{:S(2)}, u32[]{:S(2)}) %collective-permute-start.21) | collective-permute-done | bytes 393248 | tf_op jit(solution)/shard_map/ppermute | solution.py:23
  132.8 3.4 %shard_map.68 = bf16[3072,768]{1,0:T(8,128)(2,1)S(1)} custom-call(s32[5]{0:T(128)S(1)} %copy-done.8, bf16[512,768]{1,0:T(8,128)(2,1)S(1)} %collective-permute-done.18.g, bf16[2,1536,256]{2,1,0:T(8,128)(2,1)S(1)} %bitcast.37, bf16[2,1536,256]{2,1,0:T(8,128)(2,1)S(1)} %bitcast.41, bf16[3072,768]{1,0:T(8,128)(2,1)S(1)} %shard_map.67.refs_0_), custom_call_target="tpu_custom_call" | custom-call | flops 2415919104 | bytes 16777216 | tf_op jit(solution)/shard_map/pallas_call | solution.py:261
  136.2 2.2 %copy-done.3 = bf16[3072,768]{1,0:T(8,128)(2,1)} copy-done((bf16[3072,768]{1,0:T(8,128)(2,1)}, bf16[3072,768]{1,0:T(8,128)(2,1)S(1)}, u32[]{:S(2)}) %copy-start.3) | copy-done | bytes 4718616
  138.4 2.0 %shard_map.70 = bf16[4,768,256]{2,1,0:T(8,128)(2,1)S(1)} custom-call(s32[5]{0:T(128)S(1)} %copy-done.8, bf16[512,768]{1,0:T(8,128)(2,1)S(1)} %collective-permute-done.18.g, bf16[1536,768]{1,0:T(8,128)(2,1)S(1)} %copy-done), custom_call_target="tpu_custom_call" | custom-call | flops 1207959552 | bytes 5242880 | tf_op jit(solution)/shard_map/pallas_call | solution.py:226
  140.6 2.0 %shard_map.69 = bf16[4,768,256]{2,1,0:T(8,128)(2,1)S(1)} custom-call(s32[5]{0:T(128)S(1)} %copy-done.8, bf16[512,768]{1,0:T(8,128)(2,1)S(1)} %collective-permute-done.18.g, bf16[1536,768]{1,0:T(8,128)(2,1)S(1)} %copy-done.2), custom_call_target="tpu_custom_call" | custom-call | flops 1207959552 | bytes 5242880 | tf_op jit(solution)/shard_map/pallas_call | solution.py:226
  142.6 1.2 fusion.12
  144.5 1.3 collective-permute-start.25
  146.6 2.1 %collective-permute-start.23 = (bf16[768,256]{1,0:T(8,128)(2,1)S(1)}, bf16[768,256]{1,0:T(8,128)(2,1)S(1)}, u32[]{:S(2)}, u32[]{:S(2)}) collective-permute-start(bf16[768,256]{1,0:T(8,128)(2,1)S(1)} %get-tuple-element.78), channel_id=1, source_target_pairs={{0,8},{8,0},{16,24},{24,16},{1,9},{9,1},{17,25},{25,17},{2,10},{10... | collective-permute-start | bytes 1179656 | tf_op jit(solution)/shard_map/ppermute | solution.py:23
  148.7 1.8 collective-permute-start.28
  150.5 3.4 %collective-permute-start.27 = (bf16[192,256]{1,0:T(8,128)(2,1)S(1)}, bf16[192,256]{1,0:T(8,128)(2,1)S(1)}, u32[]{:S(2)}, u32[]{:S(2)}) collective-permute-start(bf16[192,256]{1,0:T(8,128)(2,1)S(1)} %get-tuple-element.86), channel_id=1, source_target_pairs={{0,4},{2,6},{4,0},{6,2},{1,5},{3,7},{5,1},{7,3},{8,12},{10,14},{12... | collective-permute-start | bytes 294920 | tf_op jit(solution)/shard_map/ppermute | solution.py:23
  153.9 4.0 %collective-permute-done.28 = bf16[192,256]{1,0:T(8,128)(2,1)S(1)} collective-permute-done((bf16[192,256]{1,0:T(8,128)(2,1)S(1)}, bf16[192,256]{1,0:T(8,128)(2,1)S(1)}, u32[]{:S(2)}, u32[]{:S(2)}) %collective-permute-start.28) | collective-permute-done | bytes 98336 | tf_op jit(solution)/shard_map/ppermute | solution.py:23
  157.9 4.5 %collective-permute-start.26 = (bf16[192,256]{1,0:T(8,128)(2,1)S(1)}, bf16[192,256]{1,0:T(8,128)(2,1)S(1)}, u32[]{:S(2)}, u32[]{:S(2)}) collective-permute-start(bf16[192,256]{1,0:T(8,128)(2,1)S(1)} %get-tuple-element.87), channel_id=1, source_target_pairs={{0,2},{2,0},{4,6},{6,4},{1,3},{3,1},{5,7},{7,5},{8,10},{10,8},{12,... | collective-permute-start | bytes 294920 | tf_op jit(solution)/shard_map/ppermute | solution.py:23
  162.4 3.5 %collective-permute-done.26 = bf16[192,256]{1,0:T(8,128)(2,1)S(1)} collective-permute-done((bf16[192,256]{1,0:T(8,128)(2,1)S(1)}, bf16[192,256]{1,0:T(8,128)(2,1)S(1)}, u32[]{:S(2)}, u32[]{:S(2)}) %collective-permute-start.26) | collective-permute-done | bytes 98336 | tf_op jit(solution)/shard_map/ppermute | solution.py:23
  166.5 3.1 %collective-permute-start.29 = (bf16[192,256]{1,0:T(8,128)(2,1)S(1)}, bf16[192,256]{1,0:T(8,128)(2,1)S(1)}, u32[]{:S(2)}, u32[]{:S(2)}) collective-permute-start(bf16[192,256]{1,0:T(8,128)(2,1)S(1)} %get-tuple-element.82), channel_id=1, source_target_pairs={{0,2},{2,0},{4,6},{6,4},{1,3},{3,1},{5,7},{7,5},{8,10},{10,8},{12,... | collective-permute-start | bytes 294920 | tf_op jit(solution)/shard_map/ppermute | solution.py:23
  169.6 3.3 %collective-permute-start.31 = (bf16[192,256]{1,0:T(8,128)(2,1)S(1)}, bf16[192,256]{1,0:T(8,128)(2,1)S(1)}, u32[]{:S(2)}, u32[]{:S(2)}) collective-permute-start(bf16[192,256]{1,0:T(8,128)(2,1)S(1)} %get-tuple-element.83), channel_id=1, source_target_pairs={{0,6},{2,4},{4,2},{6,0},{1,7},{3,5},{5,3},{7,1},{8,14},{10,12},{12... | collective-permute-start | bytes 294920 | tf_op jit(solution)/shard_map/ppermute | solution.py:23
  173.4 3.3 %collective-permute-done.31 = bf16[192,256]{1,0:T(8,128)(2,1)S(1)} collective-permute-done((bf16[192,256]{1,0:T(8,128)(2,1)S(1)}, bf16[192,256]{1,0:T(8,128)(2,1)S(1)}, u32[]{:S(2)}, u32[]{:S(2)}) %collective-permute-start.31) | collective-permute-done | bytes 98336 | tf_op jit(solution)/shard_map/ppermute | solution.py:23
  176.7 6.7 %collective-permute-done.30 = bf16[192,256]{1,0:T(8,128)(2,1)S(1)} collective-permute-done((bf16[192,256]{1,0:T(8,128)(2,1)S(1)}, bf16[192,256]{1,0:T(8,128)(2,1)S(1)}, u32[]{:S(2)}, u32[]{:S(2)}) %collective-permute-start.30) | collective-permute-done | bytes 98336 | tf_op jit(solution)/shard_map/ppermute | solution.py:23
  183.6 3.8 %collective-permute-start.32 = (bf16[192,256]{1,0:T(8,128)(2,1)S(1)}, bf16[192,256]{1,0:T(8,128)(2,1)S(1)}, u32[]{:S(2)}, u32[]{:S(2)}) collective-permute-start(bf16[192,256]{1,0:T(8,128)(2,1)S(1)} %get-tuple-element.71), channel_id=1, source_target_pairs={{0,0},{8,8},{136,16},{128,24},{24,128},{16,136},{144,144},{152,152... | collective-permute-start | bytes 294920 | tf_op jit(solution)/shard_map/ppermute | solution.py:62
  188.2 4.0 %collective-permute-done.32 = bf16[192,256]{1,0:T(8,128)(2,1)S(1)} collective-permute-done((bf16[192,256]{1,0:T(8,128)(2,1)S(1)}, bf16[192,256]{1,0:T(8,128)(2,1)S(1)}, u32[]{:S(2)}, u32[]{:S(2)}) %collective-permute-start.32) | collective-permute-done | bytes 98336 | tf_op jit(solution)/shard_map/ppermute | solution.py:62
  (87 shorter events, 18.3 us)
Async XLA Ops:
  7.2 58.9 %all-gather.2.cloned.1.call-start = ((), (), s32[]{:S(2)}) async-start(), calls=%async_computation.1 | async-start | bytes 5898240 | tf_op jit(solution)/shard_map/all_gather | solution.py:305
  7.9 185.0 %reduce-scatter.2.cloned.1.call-start = ((), (), s32[]{:S(2)}) async-start(), calls=%async_computation.2 | async-start | bytes 5898240 | tf_op jit(solution)/shard_map/reduce_scatter | solution.py:341
  8.9 9.7 %collective-permute-start.1 = (bf16[192,256]{1,0:T(8,128)(2,1)S(1)}, bf16[192,256]{1,0:T(8,128)(2,1)S(1)}, u32[]{:S(2)}, u32[]{:S(2)}) collective-permute-start(bf16[192,256]{1,0:T(8,128)(2,1)S(1)} %get-tuple-element.92), channel_id=1, source_target_pairs={{0,0},{8,8},{16,136},{24,128},{128,24},{136,16},{144,144},{152,152... | collective-permute-start | bytes 294920 | tf_op jit(solution)/shard_map/ppermute | solution.py:58
  13.4 6.4 %collective-permute-start = (bf16[192,256]{1,0:T(8,128)(2,1)S(1)}, bf16[192,256]{1,0:T(8,128)(2,1)S(1)}, u32[]{:S(2)}, u32[]{:S(2)}) collective-permute-start(bf16[192,256]{1,0:T(8,128)(2,1)S(1)} %get-tuple-element.93), channel_id=1, source_target_pairs={{0,24},{8,16},{16,144},{24,152},{128,0},{136,8},{144,136},{152,128... | collective-permute-start | bytes 294920 | tf_op jit(solution)/shard_map/ppermute | solution.py:58
  19.8 10.8 %collective-permute-start.4 = (bf16[192,256]{1,0:T(8,128)(2,1)S(1)}, bf16[192,256]{1,0:T(8,128)(2,1)S(1)}, u32[]{:S(2)}, u32[]{:S(2)}) collective-permute-start(bf16[192,256]{1,0:T(8,128)(2,1)S(1)} %get-tuple-element.37.refs_0_), channel_id=1, source_target_pairs={{0,6},{2,4},{4,2},{6,0},{1,7},{3,5},{5,3},{7,1},{8,14},{10,12},{12... | collective-permute-start | bytes 294920 | tf_op jit(solution)/shard_map/ppermute | solution.py:23
  25.8 10.9 %collective-permute-start.3 = (bf16[192,256]{1,0:T(8,128)(2,1)S(1)}, bf16[192,256]{1,0:T(8,128)(2,1)S(1)}, u32[]{:S(2)}, u32[]{:S(2)}) collective-permute-start(bf16[192,256]{1,0:T(8,128)(2,1)S(1)} %get-tuple-element.37.refs_0_), channel_id=1, source_target_pairs={{0,4},{2,6},{4,0},{6,2},{1,5},{3,7},{5,1},{7,3},{8,12},{10,14},{12... | collective-permute-start | bytes 294920 | tf_op jit(solution)/shard_map/ppermute | solution.py:23
  26.8 9.9 %collective-permute-start.2 = (bf16[192,256]{1,0:T(8,128)(2,1)S(1)}, bf16[192,256]{1,0:T(8,128)(2,1)S(1)}, u32[]{:S(2)}, u32[]{:S(2)}) collective-permute-start(bf16[192,256]{1,0:T(8,128)(2,1)S(1)} %get-tuple-element.37.refs_0_), channel_id=1, source_target_pairs={{0,2},{2,0},{4,6},{6,4},{1,3},{3,1},{5,7},{7,5},{8,10},{10,8},{12,... | collective-permute-start | bytes 294920 | tf_op jit(solution)/shard_map/ppermute | solution.py:23
  37.3 17.2 %collective-permute-start.7 = (bf16[768,256]{1,0:T(8,128)(2,1)S(1)}, bf16[768,256]{1,0:T(8,128)(2,1)S(1)}, u32[]{:S(2)}, u32[]{:S(2)}) collective-permute-start(bf16[768,256]{1,0:T(8,128)(2,1)S(1)} %shard_map.58.refs_0_), channel_id=1, source_target_pairs={{0,24},{8,16},{16,8},{24,0},{1,25},{9,17},{17,9},{25,1},{2,26},{10... | collective-permute-start | bytes 1179656 | tf_op jit(solution)/shard_map/ppermute | solution.py:23
  37.4 17.1 %collective-permute-start.6 = (bf16[768,256]{1,0:T(8,128)(2,1)S(1)}, bf16[768,256]{1,0:T(8,128)(2,1)S(1)}, u32[]{:S(2)}, u32[]{:S(2)}) collective-permute-start(bf16[768,256]{1,0:T(8,128)(2,1)S(1)} %shard_map.58.refs_0_), channel_id=1, source_target_pairs={{0,16},{8,24},{16,0},{24,8},{1,17},{9,25},{17,1},{25,9},{2,18},{10... | collective-permute-start | bytes 1179656 | tf_op jit(solution)/shard_map/ppermute | solution.py:23
  38.5 16.6 %collective-permute-start.5 = (bf16[768,256]{1,0:T(8,128)(2,1)S(1)}, bf16[768,256]{1,0:T(8,128)(2,1)S(1)}, u32[]{:S(2)}, u32[]{:S(2)}) collective-permute-start(bf16[768,256]{1,0:T(8,128)(2,1)S(1)} %shard_map.58.refs_0_), channel_id=1, source_target_pairs={{0,8},{8,0},{16,24},{24,16},{1,9},{9,1},{17,25},{25,17},{2,10},{10... | collective-permute-start | bytes 1179656 | tf_op jit(solution)/shard_map/ppermute | solution.py:23
  41.4 6.8 %collective-permute-start.10 = (bf16[192,256]{1,0:T(8,128)(2,1)S(1)}, bf16[192,256]{1,0:T(8,128)(2,1)S(1)}, u32[]{:S(2)}, u32[]{:S(2)}) collective-permute-start(bf16[192,256]{1,0:T(8,128)(2,1)S(1)} %get-tuple-element.42.refs_0_), channel_id=1, source_target_pairs={{0,6},{2,4},{4,2},{6,0},{1,7},{3,5},{5,3},{7,1},{8,14},{10,12},{12... | collective-permute-start | bytes 294920 | tf_op jit(solution)/shard_map/ppermute | solution.py:23
  44.5 9.6 %collective-permute-start.9 = (bf16[192,256]{1,0:T(8,128)(2,1)S(1)}, bf16[192,256]{1,0:T(8,128)(2,1)S(1)}, u32[]{:S(2)}, u32[]{:S(2)}) collective-permute-start(bf16[192,256]{1,0:T(8,128)(2,1)S(1)} %get-tuple-element.42.refs_0_), channel_id=1, source_target_pairs={{0,4},{2,6},{4,0},{6,2},{1,5},{3,7},{5,1},{7,3},{8,12},{10,14},{12... | collective-permute-start | bytes 294920 | tf_op jit(solution)/shard_map/ppermute | solution.py:23
  48.2 6.2 %collective-permute-start.8 = (bf16[192,256]{1,0:T(8,128)(2,1)S(1)}, bf16[192,256]{1,0:T(8,128)(2,1)S(1)}, u32[]{:S(2)}, u32[]{:S(2)}) collective-permute-start(bf16[192,256]{1,0:T(8,128)(2,1)S(1)} %get-tuple-element.42.refs_0_), channel_id=1, source_target_pairs={{0,2},{2,0},{4,6},{6,4},{1,3},{3,1},{5,7},{7,5},{8,10},{10,8},{12,... | collective-permute-start | bytes 294920 | tf_op jit(solution)/shard_map/ppermute | solution.py:23
  55.8 10.2 %copy-start.4 = (bf16[3072,256]{1,0:T(8,128)(2,1)}, bf16[3072,256]{1,0:T(8,128)(2,1)S(1)}, u32[]{:S(2)}) copy-start(bf16[3072,256]{1,0:T(8,128)(2,1)S(1)} %shard_map.60) | copy-start | bytes 4718596
  55.9 5.5 %collective-permute-start.14 = (bf16[3072,256]{1,0:T(8,128)(2,1)S(1)}, bf16[3072,256]{1,0:T(8,128)(2,1)S(1)}, u32[]{:S(2)}, u32[]{:S(2)}) collective-permute-start(bf16[3072,256]{1,0:T(8,128)(2,1)S(1)} %shard_map.60), channel_id=1, source_target_pairs={{0,1},{1,0},{2,3},{3,2},{4,5},{5,4},{6,7},{7,6},{8,9},{9,8},{10,11... | collective-permute-start | bytes 4718600 | tf_op jit(solution)/shard_map/ppermute | solution.py:23
  56.5 21.3 %collective-permute-start.13 = (bf16[768,256]{1,0:T(8,128)(2,1)S(1)}, bf16[768,256]{1,0:T(8,128)(2,1)}, u32[]{:S(2)}, u32[]{:S(2)}) collective-permute-start(bf16[768,256]{1,0:T(8,128)(2,1)S(1)} %shard_map.59.refs_0_), channel_id=1, source_target_pairs={{0,24},{8,16},{16,8},{24,0},{1,25},{9,17},{17,9},{25,1},{2,26},{10... | collective-permute-start | bytes 1179656 | tf_op jit(solution)/shard_map/ppermute | solution.py:23
  59.2 18.6 %collective-permute-start.12 = (bf16[768,256]{1,0:T(8,128)(2,1)S(1)}, bf16[768,256]{1,0:T(8,128)(2,1)}, u32[]{:S(2)}, u32[]{:S(2)}) collective-permute-start(bf16[768,256]{1,0:T(8,128)(2,1)S(1)} %shard_map.59.refs_0_), channel_id=1, source_target_pairs={{0,16},{8,24},{16,0},{24,8},{1,17},{9,25},{17,1},{25,9},{2,18},{10... | collective-permute-start | bytes 1179656 | tf_op jit(solution)/shard_map/ppermute | solution.py:23
  59.8 18.6 %collective-permute-start.11 = (bf16[768,256]{1,0:T(8,128)(2,1)S(1)}, bf16[768,256]{1,0:T(8,128)(2,1)}, u32[]{:S(2)}, u32[]{:S(2)}) collective-permute-start(bf16[768,256]{1,0:T(8,128)(2,1)S(1)} %shard_map.59.refs_0_), channel_id=1, source_target_pairs={{0,8},{8,0},{16,24},{24,16},{1,9},{9,1},{17,25},{25,17},{2,10},{10... | collective-permute-start | bytes 1179656 | tf_op jit(solution)/shard_map/ppermute | solution.py:23
  61.3 4.7 %copy-start.6 = (bf16[3072,256]{1,0:T(8,128)(2,1)}, bf16[3072,256]{1,0:T(8,128)(2,1)S(1)}, u32[]{:S(2)}) copy-start(bf16[3072,256]{1,0:T(8,128)(2,1)S(1)} %collective-permute-done.14) | copy-start | bytes 4718596
  78.4 5.4 %copy-start.1 = (bf16[1536,768]{1,0:T(8,128)(2,1)S(1)}, bf16[1536,768]{1,0:T(8,128)(2,1)}, u32[]{:S(2)}) copy-start(bf16[1536,768]{1,0:T(8,128)(2,1)} %get-tuple-element.56.w) | copy-start | bytes 7077892
  78.4 5.4 %copy-start.8 = (s32[5]{0:T(128)S(1)}, s32[5]{0:T(128)}, u32[]{:S(2)}) copy-start(s32[5]{0:T(128)} %stack.23.idx) | copy-start | bytes 64
  80.1 5.8 %collective-permute-start.15 = (bf16[3072,256]{1,0:T(8,128)(2,1)S(1)}, bf16[3072,256]{1,0:T(8,128)(2,1)S(1)}, u32[]{:S(2)}, u32[]{:S(2)}) collective-permute-start(bf16[3072,256]{1,0:T(8,128)(2,1)S(1)} %shard_map.62), channel_id=1, source_target_pairs={{0,1},{1,0},{2,3},{3,2},{4,5},{5,4},{6,7},{7,6},{8,9},{9,8},{10,11... | collective-permute-start | bytes 4718600 | tf_op jit(solution)/shard_map/ppermute | solution.py:23
  80.2 21.6 %collective-permute-start.16 = (bf16[512,768]{1,0:T(8,128)(2,1)S(1)}, bf16[512,768]{1,0:T(8,128)(2,1)S(1)}, u32[]{:S(2)}, u32[]{:S(2)}) collective-permute-start(bf16[512,768]{1,0:T(8,128)(2,1)S(1)} %copy-done.15), channel_id=1, source_target_pairs={{0,128},{128,0},{1,129},{129,1},{2,130},{130,2},{3,131},{131,3},{4... | collective-permute-start | bytes 2359304 | tf_op jit(solution)/shard_map/ppermute | solution.py:23
  85.9 15.9 %copy-start.10 = (bf16[512,768]{1,0:T(8,128)(2,1)S(1)}, bf16[512,768]{1,0:T(8,128)(2,1)}, u32[]{:S(2)}) copy-start(bf16[512,768]{1,0:T(8,128)(2,1)} %param.5) | copy-start | bytes 2359300
  106.0 4.0 %collective-permute-start.17 = (bf16[4,768,256]{2,1,0:T(8,128)(2,1)S(1)}, bf16[4,768,256]{2,1,0:T(8,128)(2,1)S(1)}, u32[]{:S(2)}, u32[]{:S(2)}) collective-permute-start(bf16[4,768,256]{2,1,0:T(8,128)(2,1)S(1)} %shard_map.66), channel_id=1, source_target_pairs={{0,1},{1,0},{2,3},{3,2},{4,5},{5,4},{6,7},{7,6},{8,9},{9,8},{10,11... | collective-permute-start | bytes 4718600 | tf_op jit(solution)/shard_map/ppermute | solution.py:23
  106.1 20.0 %collective-permute-start.18 = (bf16[512,768]{1,0:T(8,128)(2,1)S(1)}, bf16[512,768]{1,0:T(8,128)(2,1)S(1)}, u32[]{:S(2)}, u32[]{:S(2)}) collective-permute-start(bf16[512,768]{1,0:T(8,128)(2,1)S(1)} %get-tuple-element.74.g), channel_id=1, source_target_pairs={{0,128},{128,0},{1,129},{129,1},{2,130},{130,2},{3,131},{131,3},{4... | collective-permute-start | bytes 2359304 | tf_op jit(solution)/shard_map/ppermute | solution.py:23
  110.3 7.6 %copy-start.9 = (bf16[4,768,256]{2,1,0:T(8,128)(2,1)}, bf16[4,768,256]{2,1,0:T(8,128)(2,1)S(1)}, u32[]{:S(2)}) copy-start(bf16[4,768,256]{2,1,0:T(8,128)(2,1)S(1)} %add_convert_fusion.1) | copy-start | bytes 4718596
  110.4 20.9 %collective-permute-start.21 = (bf16[768,256]{1,0:T(8,128)(2,1)S(1)}, bf16[768,256]{1,0:T(8,128)(2,1)S(1)}, u32[]{:S(2)}, u32[]{:S(2)}) collective-permute-start(bf16[768,256]{1,0:T(8,128)(2,1)S(1)} %get-tuple-element.79), channel_id=1, source_target_pairs={{0,24},{8,16},{16,8},{24,0},{1,25},{9,17},{17,9},{25,1},{2,26},{10... | collective-permute-start | bytes 1179656 | tf_op jit(solution)/shard_map/ppermute | solution.py:23
  111.7 19.6 %collective-permute-start.20 = (bf16[768,256]{1,0:T(8,128)(2,1)S(1)}, bf16[768,256]{1,0:T(8,128)(2,1)S(1)}, u32[]{:S(2)}, u32[]{:S(2)}) collective-permute-start(bf16[768,256]{1,0:T(8,128)(2,1)S(1)} %get-tuple-element.80), channel_id=1, source_target_pairs={{0,16},{8,24},{16,0},{24,8},{1,17},{9,25},{17,1},{25,9},{2,18},{10... | collective-permute-start | bytes 1179656 | tf_op jit(solution)/shard_map/ppermute | solution.py:23
  112.7 20.2 %copy-start.5 = (bf16[3072,256]{1,0:T(8,128)(2,1)S(1)}, bf16[3072,256]{1,0:T(8,128)(2,1)}, u32[]{:S(2)}) copy-start(bf16[3072,256]{1,0:T(8,128)(2,1)} %copy-done.4) | copy-start | bytes 4718596
  112.7 20.2 %copy-start.7 = (bf16[3072,256]{1,0:T(8,128)(2,1)S(1)}, bf16[3072,256]{1,0:T(8,128)(2,1)}, u32[]{:S(2)}) copy-start(bf16[3072,256]{1,0:T(8,128)(2,1)} %copy-done.6) | copy-start | bytes 4718596
  112.7 19.4 %collective-permute-start.19 = (bf16[768,256]{1,0:T(8,128)(2,1)S(1)}, bf16[768,256]{1,0:T(8,128)(2,1)S(1)}, u32[]{:S(2)}, u32[]{:S(2)}) collective-permute-start(bf16[768,256]{1,0:T(8,128)(2,1)S(1)} %get-tuple-element.81), channel_id=1, source_target_pairs={{0,8},{8,0},{16,24},{24,16},{1,9},{9,1},{17,25},{25,17},{2,10},{10... | collective-permute-start | bytes 1179656 | tf_op jit(solution)/shard_map/ppermute | solution.py:23
  136.2 2.2 %copy-start.3 = (bf16[3072,768]{1,0:T(8,128)(2,1)}, bf16[3072,768]{1,0:T(8,128)(2,1)S(1)}, u32[]{:S(2)}) copy-start(bf16[3072,768]{1,0:T(8,128)(2,1)S(1)} %shard_map.68) | copy-start | bytes 14155780
  138.4 2.2 %copy-start.2 = (bf16[1536,768]{1,0:T(8,128)(2,1)S(1)}, bf16[1536,768]{1,0:T(8,128)(2,1)}, u32[]{:S(2)}) copy-start(bf16[1536,768]{1,0:T(8,128)(2,1)} %get-tuple-element.56.w) | copy-start | bytes 7077892
  140.5 2.2 %copy-start.12 = (bf16[768,256]{1,0:T(8,128)(2,1)S(1)}, bf16[768,256]{1,0:T(8,128)(2,1)}, u32[]{:S(2)}) copy-start(bf16[768,256]{1,0:T(8,128)(2,1)} %copy-done.11) | copy-start | bytes 1179652
  140.5 2.2 %copy-start.14 = (bf16[768,256]{1,0:T(8,128)(2,1)S(1)}, bf16[768,256]{1,0:T(8,128)(2,1)}, u32[]{:S(2)}) copy-start(bf16[768,256]{1,0:T(8,128)(2,1)} %copy-done.13) | copy-start | bytes 1179652
  140.5 3.5 %collective-permute-start.22 = (bf16[4,768,256]{2,1,0:T(8,128)(2,1)S(1)}, bf16[4,768,256]{2,1,0:T(8,128)(2,1)S(1)}, u32[]{:S(2)}, u32[]{:S(2)}) collective-permute-start(bf16[4,768,256]{2,1,0:T(8,128)(2,1)S(1)} %shard_map.70), channel_id=1, source_target_pairs={{0,1},{1,0},{2,3},{3,2},{4,5},{5,4},{6,7},{7,6},{8,9},{9,8},{10,11... | collective-permute-start | bytes 4718600 | tf_op jit(solution)/shard_map/ppermute | solution.py:23
  144.5 21.4 %collective-permute-start.25 = (bf16[768,256]{1,0:T(8,128)(2,1)S(1)}, bf16[768,256]{1,0:T(8,128)(2,1)S(1)}, u32[]{:S(2)}, u32[]{:S(2)}) collective-permute-start(bf16[768,256]{1,0:T(8,128)(2,1)S(1)} %get-tuple-element.76), channel_id=1, source_target_pairs={{0,24},{8,16},{16,8},{24,0},{1,25},{9,17},{17,9},{25,1},{2,26},{10... | collective-permute-start | bytes 1179656 | tf_op jit(solution)/shard_map/ppermute | solution.py:23
  145.8 20.1 %collective-permute-start.24 = (bf16[768,256]{1,0:T(8,128)(2,1)S(1)}, bf16[768,256]{1,0:T(8,128)(2,1)S(1)}, u32[]{:S(2)}, u32[]{:S(2)}) collective-permute-start(bf16[768,256]{1,0:T(8,128)(2,1)S(1)} %get-tuple-element.77), channel_id=1, source_target_pairs={{0,16},{8,24},{16,0},{24,8},{1,17},{9,25},{17,1},{25,9},{2,18},{10... | collective-permute-start | bytes 1179656 | tf_op jit(solution)/shard_map/ppermute | solution.py:23
  146.6 19.6 %collective-permute-start.23 = (bf16[768,256]{1,0:T(8,128)(2,1)S(1)}, bf16[768,256]{1,0:T(8,128)(2,1)S(1)}, u32[]{:S(2)}, u32[]{:S(2)}) collective-permute-start(bf16[768,256]{1,0:T(8,128)(2,1)S(1)} %get-tuple-element.78), channel_id=1, source_target_pairs={{0,8},{8,0},{16,24},{24,16},{1,9},{9,1},{17,25},{25,17},{2,10},{10... | collective-permute-start | bytes 1179656 | tf_op jit(solution)/shard_map/ppermute | solution.py:23
  148.7 9.2 %collective-permute-start.28 = (bf16[192,256]{1,0:T(8,128)(2,1)S(1)}, bf16[192,256]{1,0:T(8,128)(2,1)S(1)}, u32[]{:S(2)}, u32[]{:S(2)}) collective-permute-start(bf16[192,256]{1,0:T(8,128)(2,1)S(1)} %get-tuple-element.85), channel_id=1, source_target_pairs={{0,6},{2,4},{4,2},{6,0},{1,7},{3,5},{5,3},{7,1},{8,14},{10,12},{12... | collective-permute-start | bytes 294920 | tf_op jit(solution)/shard_map/ppermute | solution.py:23
  150.5 12.0 %collective-permute-start.27 = (bf16[192,256]{1,0:T(8,128)(2,1)S(1)}, bf16[192,256]{1,0:T(8,128)(2,1)S(1)}, u32[]{:S(2)}, u32[]{:S(2)}) collective-permute-start(bf16[192,256]{1,0:T(8,128)(2,1)S(1)} %get-tuple-element.86), channel_id=1, source_target_pairs={{0,4},{2,6},{4,0},{6,2},{1,5},{3,7},{5,1},{7,3},{8,12},{10,14},{12... | collective-permute-start | bytes 294920 | tf_op jit(solution)/shard_map/ppermute | solution.py:23
  157.9 8.0 %collective-permute-start.26 = (bf16[192,256]{1,0:T(8,128)(2,1)S(1)}, bf16[192,256]{1,0:T(8,128)(2,1)S(1)}, u32[]{:S(2)}, u32[]{:S(2)}) collective-permute-start(bf16[192,256]{1,0:T(8,128)(2,1)S(1)} %get-tuple-element.87), channel_id=1, source_target_pairs={{0,2},{2,0},{4,6},{6,4},{1,3},{3,1},{5,7},{7,5},{8,10},{10,8},{12,... | collective-permute-start | bytes 294920 | tf_op jit(solution)/shard_map/ppermute | solution.py:23
  166.5 6.9 %collective-permute-start.29 = (bf16[192,256]{1,0:T(8,128)(2,1)S(1)}, bf16[192,256]{1,0:T(8,128)(2,1)S(1)}, u32[]{:S(2)}, u32[]{:S(2)}) collective-permute-start(bf16[192,256]{1,0:T(8,128)(2,1)S(1)} %get-tuple-element.82), channel_id=1, source_target_pairs={{0,2},{2,0},{4,6},{6,4},{1,3},{3,1},{5,7},{7,5},{8,10},{10,8},{12,... | collective-permute-start | bytes 294920 | tf_op jit(solution)/shard_map/ppermute | solution.py:23
  169.6 7.0 %collective-permute-start.31 = (bf16[192,256]{1,0:T(8,128)(2,1)S(1)}, bf16[192,256]{1,0:T(8,128)(2,1)S(1)}, u32[]{:S(2)}, u32[]{:S(2)}) collective-permute-start(bf16[192,256]{1,0:T(8,128)(2,1)S(1)} %get-tuple-element.83), channel_id=1, source_target_pairs={{0,6},{2,4},{4,2},{6,0},{1,7},{3,5},{5,3},{7,1},{8,14},{10,12},{12... | collective-permute-start | bytes 294920 | tf_op jit(solution)/shard_map/ppermute | solution.py:23
  172.9 10.4 %collective-permute-start.30 = (bf16[192,256]{1,0:T(8,128)(2,1)S(1)}, bf16[192,256]{1,0:T(8,128)(2,1)S(1)}, u32[]{:S(2)}, u32[]{:S(2)}) collective-permute-start(bf16[192,256]{1,0:T(8,128)(2,1)S(1)} %get-tuple-element.84), channel_id=1, source_target_pairs={{0,4},{2,6},{4,0},{6,2},{1,5},{3,7},{5,1},{7,3},{8,12},{10,14},{12... | collective-permute-start | bytes 294920 | tf_op jit(solution)/shard_map/ppermute | solution.py:23
  183.5 4.7 %collective-permute-start.33 = (bf16[192,256]{1,0:T(8,128)(2,1)S(1)}, bf16[192,256]{1,0:T(8,128)(2,1)S(1)}, u32[]{:S(2)}, u32[]{:S(2)}) collective-permute-start(bf16[192,256]{1,0:T(8,128)(2,1)S(1)} %broadcast_select_fusion.4), channel_id=1, source_target_pairs={{24,0},{16,8},{144,16},{152,24},{0,128},{8,136},{136,144},{128,152... | collective-permute-start | bytes 294920 | tf_op jit(solution)/shard_map/ppermute | solution.py:62
  183.6 8.6 %collective-permute-start.32 = (bf16[192,256]{1,0:T(8,128)(2,1)S(1)}, bf16[192,256]{1,0:T(8,128)(2,1)S(1)}, u32[]{:S(2)}, u32[]{:S(2)}) collective-permute-start(bf16[192,256]{1,0:T(8,128)(2,1)S(1)} %get-tuple-element.71), channel_id=1, source_target_pairs={{0,0},{8,8},{136,16},{128,24},{24,128},{16,136},{144,144},{152,152... | collective-permute-start | bytes 294920 | tf_op jit(solution)/shard_map/ppermute | solution.py:62
  (4 other events, 5.2 us)
Sparse Core Ops, SparseCore 0:
  9.8 56.2 all-gather.1
  138.5 50.7 reduce-scatter.1

commit v3 on v2

--- a/solution.py
+++ b/solution.py
@@ -117,7 +117,7 @@
     return idx[2] >> 1
 
 
-def project_kernel(idx, own, other, w, out, w0, w1, a_v, w_v, acc, a_sems, w_sems, out_sems):
+def project_kernel(idx, own, other, w, top, low, w0, w1, a_v, w_v, acc, a_sems, w_sems, out_sems):
     loads = [
         pltpu.make_async_copy(a, a_v.at[dc], a_sems.at[dc]) for dc, a in enumerate((own, other))
     ]
@@ -157,7 +157,7 @@
             if step < 3:
                 acc[half] = part
             else:
-                out[half * n : half * n + n] = part.astype(BF16)
+                (top, low)[half][...] = part.astype(BF16)
     for store in stores:
         store.wait()
 
@@ -166,10 +166,10 @@
     width = own.shape[-1]
     return call(
         project_kernel,
-        [jax.ShapeDtypeStruct((2 * width, 768), BF16)]
+        [jax.ShapeDtypeStruct((width, 768), BF16)] * 2
         + [jax.ShapeDtypeStruct((1536, 768), BF16)] * 2,
         [SMEM, HBM, HBM, HBM],
-        [VMEM, HBM, HBM],
+        [VMEM, VMEM, HBM, HBM],
         [
             pltpu.VMEM((2, 2, 1536, width), BF16),
             pltpu.VMEM((2, 1536, 768), BF16),
@@ -320,13 +320,14 @@
     own_p = in_order(planes_p)
     planes_o = gather_pieces(join(*pieces_o), "y")
     other_p = flip(own_p, "c", 1)
-    send, w0, w1 = project(idx, own_p, other_p, w_all)
-    came = over_z(send)
-    *planes_o, w0 = stage(*planes_o, w0)
+    top, low, w0, w1 = project(idx, own_p, other_p, w_all)
+    *planes_o, came_top = stage(*planes_o, over_z(top))
+    came_low = over_z(low)
 
     own_o = in_order(planes_o)
     other_o = flip(own_o, "c", 1)
     pre_act = project_half(idx, other_o, w1, [project_half(idx, own_o, w0, [])])
+    came = jnp.concatenate([came_top, came_low])
     activated, grad_o = gelu_pair(added(pre_act, [came]), grad_out)
     grad_p = over_z(grad_o)
 
@@ -334,10 +335,10 @@
     both_o = added(input_grad(idx, grad_o, w0), [half]).astype(BF16)
     rows_o = [flip(both_o[d], "y", d) for d in (1, 2, 3)]
     partial = weight_grad(idx, grad_o, own_o, other_o, [])
-    grad_p, partial, *rows_o = stage(grad_p, partial, *rows_o)
+    grad_p, partial, rows_o[0], rows_o[2] = stage(grad_p, partial, rows_o[0], rows_o[2])
 
     partial = weight_grad(idx, grad_p, own_p, other_p, [partial])
-    partial, grad_p = stage(partial, grad_p)
+    partial, grad_p, rows_o[1] = stage(partial, grad_p, rows_o[1])
     grad_weight = lax.psum_scatter(partial, "x", scatter_dimension=0, tiled=True)
     half = flip(input_grad(idx, grad_p, w1), "c", 1)
     both_p = added(input_grad(idx, grad_p, w0), [half]).astype(BF16)

time: 200 us -> 193 us (0.965)
  waiting for transfers between devices: 81.4 us -> 65.6 us
  starting transfers between devices: 63 us -> 66.9 us
  local copies, waits for them, and re-layouts: 4.54 us -> 7.8 us
    ppermute x30 -> x31, waiting for transfers between devices: 64.9 us -> 54 us  [flip(): lax.ppermute(value, axis, [(i, i ^ mask) for i in range(SIZES[axis])])]
    all_gather x1, waiting for transfers between devices: 4.74 us -> 0.95 us  [per_device(): w_all = lax.all_gather(weight, 'x', axis=0, tiled=True)]
    unnamed x32 -> x44, local copies, waits for them, and re-layouts: 3.72 us -> 6.79 us
    ppermute x30 -> x31, starting transfers between devices: 54.5 us -> 57.2 us  [flip(): lax.ppermute(value, axis, [(i, i ^ mask) for i in range(SIZES[axis])])]
  transfers between devices with their start and end apart: 36 -> 37, of which waited for: 22 -> 21; matrix products, arithmetic and copies ran while one was open for 2% -> 3% of each run, Pallas kernels for 12% -> 14%
where the time goes in v3:
time: 193 us; the launch traced here: 191 us
  starting transfers between devices  66.9 us (35%)
  waiting for transfers between devices  65.6 us (34%)
  Pallas kernels  30.1 us (16%)
  between operations  14.5 us (8%)
  local copies, waits for them, and re-layouts  7.8 us (4%)
  other arithmetic  6.46 us (3%)
    ppermute x31, starting transfers between devices, flip(): lax.ppermute(value, axis, [(i, i ^ mask) for i in range(SIZES[axis])])  57.2 us
    ppermute x31, waiting for transfers between devices, flip(): lax.ppermute(value, axis, [(i, i ^ mask) for i in range(SIZES[axis])])  54 us
    pallas_call x4, Pallas kernels, input_grad(): call(input_grad_kernel, jax.ShapeDtypeStruct((4, 768, width), BF16), [SME...  8.14 us
    pallas_call x1, Pallas kernels, project(): call(project_kernel, [jax.ShapeDtypeStruct((width, 768), BF16)] * 2 + [ja...  7.97 us
    unnamed x44, local copies, waits for them, and re-layouts  6.79 us
    pallas_call x2, Pallas kernels, weight_grad(): call(weight_grad_kernel, jax.ShapeDtypeStruct((3072, 768), BF16), [SMEM]...  6.69 us
    ppermute x2, waiting for transfers between devices, spread(): return lax.ppermute(value, ('zl', 'y'), spread_pairs(turn))  6.33 us
    ppermute x2, starting transfers between devices, spread_back(): lax.ppermute(value, ('zl', 'y'), [(b, a) for a, b in spread_pairs(turn)])  5.05 us
  transfers between devices with their start and end apart: 37, of which 21 were waited for; matrix products, arithmetic and copies ran while one was open for 3% of the time, Pallas kernels for 14%

profile of v3, /device:TPU:38, one launch (start us, length us, event | category | flops | bytes accessed | tf_op | source)
XLA Modules:
  0.0 191.4 jit_solution(17832554857521994105)
XLA Ops:
  8.9 4.5 %collective-permute-start.1 = (bf16[192,256]{1,0:T(8,128)(2,1)S(1)}, bf16[192,256]{1,0:T(8,128)(2,1)S(1)}, u32[]{:S(2)}, u32[]{:S(2)}) collective-permute-start(bf16[192,256]{1,0:T(8,128)(2,1)S(1)} %get-tuple-element.94), channel_id=1, source_target_pairs={{0,0},{8,8},{16,136},{24,128},{128,24},{136,16},{144,144},{152,152... | collective-permute-start | bytes 294920 | tf_op jit(solution)/shard_map/ppermute | solution.py:58
  13.5 5.1 %collective-permute-done.1 = bf16[192,256]{1,0:T(8,128)(2,1)S(1)} collective-permute-done((bf16[192,256]{1,0:T(8,128)(2,1)S(1)}, bf16[192,256]{1,0:T(8,128)(2,1)S(1)}, u32[]{:S(2)}, u32[]{:S(2)}) %collective-permute-start.1) | collective-permute-done | bytes 98336 | tf_op jit(solution)/shard_map/ppermute | solution.py:58
  19.9 5.9 %collective-permute-start.4 = (bf16[192,256]{1,0:T(8,128)(2,1)S(1)}, bf16[192,256]{1,0:T(8,128)(2,1)S(1)}, u32[]{:S(2)}, u32[]{:S(2)}) collective-permute-start(bf16[192,256]{1,0:T(8,128)(2,1)S(1)} %get-tuple-element.38.refs_0_), channel_id=1, source_target_pairs={{0,6},{2,4},{4,2},{6,0},{1,7},{3,5},{5,3},{7,1},{8,14},{10,12},{12... | collective-permute-start | bytes 294920 | tf_op jit(solution)/shard_map/ppermute | solution.py:23
  26.8 1.5 collective-permute-start.2
  28.3 2.5 %collective-permute-done.4.refs_3_ = bf16[192,256]{1,0:T(8,128)(2,1)S(1)} collective-permute-done((bf16[192,256]{1,0:T(8,128)(2,1)S(1)}, bf16[192,256]{1,0:T(8,128)(2,1)S(1)}, u32[]{:S(2)}, u32[]{:S(2)}) %collective-permute-start.4) | collective-permute-done | bytes 98336 | tf_op jit(solution)/shard_map/ppermute | solution.py:23
  30.7 6.0 %collective-permute-done.3.refs_2_ = bf16[192,256]{1,0:T(8,128)(2,1)S(1)} collective-permute-done((bf16[192,256]{1,0:T(8,128)(2,1)S(1)}, bf16[192,256]{1,0:T(8,128)(2,1)S(1)}, u32[]{:S(2)}, u32[]{:S(2)}) %collective-permute-start.3) | collective-permute-done | bytes 98336 | tf_op jit(solution)/shard_map/ppermute | solution.py:23
  38.5 3.0 %collective-permute-start.5 = (bf16[768,256]{1,0:T(8,128)(2,1)S(1)}, bf16[768,256]{1,0:T(8,128)(2,1)S(1)}, u32[]{:S(2)}, u32[]{:S(2)}) collective-permute-start(bf16[768,256]{1,0:T(8,128)(2,1)S(1)} %shard_map.58.refs_0_), channel_id=1, source_target_pairs={{0,8},{8,0},{16,24},{24,16},{1,9},{9,1},{17,25},{25,17},{2,10},{10... | collective-permute-start | bytes 1179656 | tf_op jit(solution)/shard_map/ppermute | solution.py:23
  41.4 3.1 %collective-permute-start.10 = (bf16[192,256]{1,0:T(8,128)(2,1)S(1)}, bf16[192,256]{1,0:T(8,128)(2,1)S(1)}, u32[]{:S(2)}, u32[]{:S(2)}) collective-permute-start(bf16[192,256]{1,0:T(8,128)(2,1)S(1)} %get-tuple-element.43.refs_0_), channel_id=1, source_target_pairs={{0,6},{2,4},{4,2},{6,0},{1,7},{3,5},{5,3},{7,1},{8,14},{10,12},{12... | collective-permute-start | bytes 294920 | tf_op jit(solution)/shard_map/ppermute | solution.py:23
  44.5 2.1 %collective-permute-start.9 = (bf16[192,256]{1,0:T(8,128)(2,1)S(1)}, bf16[192,256]{1,0:T(8,128)(2,1)S(1)}, u32[]{:S(2)}, u32[]{:S(2)}) collective-permute-start(bf16[192,256]{1,0:T(8,128)(2,1)S(1)} %get-tuple-element.43.refs_0_), channel_id=1, source_target_pairs={{0,4},{2,6},{4,0},{6,2},{1,5},{3,7},{5,1},{7,3},{8,12},{10,14},{12... | collective-permute-start | bytes 294920 | tf_op jit(solution)/shard_map/ppermute | solution.py:23
  46.7 1.6 collective-permute-done.10.refs_3_
  48.2 1.6 collective-permute-start.8
  49.8 4.3 %collective-permute-done.9.refs_2_ = bf16[192,256]{1,0:T(8,128)(2,1)S(1)} collective-permute-done((bf16[192,256]{1,0:T(8,128)(2,1)S(1)}, bf16[192,256]{1,0:T(8,128)(2,1)S(1)}, u32[]{:S(2)}, u32[]{:S(2)}) %collective-permute-start.9) | collective-permute-done | bytes 98336 | tf_op jit(solution)/shard_map/ppermute | solution.py:23
  60.9 2.7 %collective-permute-start.13 = (bf16[768,256]{1,0:T(8,128)(2,1)S(1)}, bf16[768,256]{1,0:T(8,128)(2,1)}, u32[]{:S(2)}, u32[]{:S(2)}) collective-permute-start(bf16[768,256]{1,0:T(8,128)(2,1)S(1)} %shard_map.59.refs_0_), channel_id=1, source_target_pairs={{0,24},{8,16},{16,8},{24,0},{1,25},{9,17},{17,9},{25,1},{2,26},{10... | collective-permute-start | bytes 1179656 | tf_op jit(solution)/shard_map/ppermute | solution.py:23
  66.3 8.0 %shard_map.61 = (bf16[256,768]{1,0:T(8,128)(2,1)}, bf16[256,768]{1,0:T(8,128)(2,1)}, bf16[1536,768]{1,0:T(8,128)(2,1)}, bf16[1536,768]{1,0:T(8,128)(2,1)}) custom-call(s32[5]{0:T(128)} %stack.23.idx, bf16[2,1536,256]{2,1,0:T(8,128)(2,1)} %bitcast.36, bf16[2,1536,256]{2,1,0:T(8,128)(2,1)} %bitcast.40, bf16[3072,768]{1,0:T(8,128)(2,1)} %all-gather.2.cloned.1.call-done.w), custom_call_target="tpu_custom_call" | custom-call | flops 2415919104 | bytes 20971520 | tf_op jit(solution)/shard_map/pallas_call | solution.py:167
  74.3 3.5 %collective-permute-start.15 = (bf16[256,768]{1,0:T(8,128)(2,1)}, bf16[256,768]{1,0:T(8,128)(2,1)S(1)}, u32[]{:S(2)}, u32[]{:S(2)}) collective-permute-start(bf16[256,768]{1,0:T(8,128)(2,1)} %get-tuple-element.51), channel_id=1, source_target_pairs={{0,128},{128,0},{1,129},{129,1},{2,130},{130,2},{3,131},{131,3},{4... | collective-permute-start | bytes 1179656 | tf_op jit(solution)/shard_map/ppermute | solution.py:23
  77.9 4.2 %collective-permute-done.13.refs_2_ = bf16[768,256]{1,0:T(8,128)(2,1)} collective-permute-done((bf16[768,256]{1,0:T(8,128)(2,1)S(1)}, bf16[768,256]{1,0:T(8,128)(2,1)}, u32[]{:S(2)}, u32[]{:S(2)}) %collective-permute-start.13) | collective-permute-done | bytes 393248 | tf_op jit(solution)/shard_map/ppermute | solution.py:23
  82.7 4.1 %collective-permute-done.15 = bf16[256,768]{1,0:T(8,128)(2,1)S(1)} collective-permute-done((bf16[256,768]{1,0:T(8,128)(2,1)}, bf16[256,768]{1,0:T(8,128)(2,1)S(1)}, u32[]{:S(2)}, u32[]{:S(2)}) %collective-permute-start.15) | collective-permute-done | bytes 393248 | tf_op jit(solution)/shard_map/ppermute | solution.py:23
  86.9 1.4 shard_map.62
  88.4 2.0 %collective-permute-start.17 = (bf16[256,768]{1,0:T(8,128)(2,1)S(1)}, bf16[256,768]{1,0:T(8,128)(2,1)S(1)}, u32[]{:S(2)}, u32[]{:S(2)}) collective-permute-start(bf16[256,768]{1,0:T(8,128)(2,1)S(1)} %copy-done.21), channel_id=1, source_target_pairs={{0,128},{128,0},{1,129},{129,1},{2,130},{130,2},{3,131},{131,3},{4... | collective-permute-start | bytes 1179656 | tf_op jit(solution)/shard_map/ppermute | solution.py:23
  90.5 2.0 %shard_map.63.refs_0_ = f32[512,768]{1,0:T(8,128)S(1)} custom-call(s32[5]{0:T(128)S(1)} %copy-done.16, bf16[2,1536,256]{2,1,0:T(8,128)(2,1)S(1)} %bitcast.34, bf16[1536,768]{1,0:T(8,128)(2,1)S(1)} %copy-done.1), custom_call_target="tpu_custom_call" | custom-call | flops 1207959552 | bytes 5242880 | tf_op jit(solution)/shard_map/pallas_call | solution.py:198
  92.5 2.0 %shard_map.64 = f32[512,768]{1,0:T(8,128)S(1)} custom-call(s32[5]{0:T(128)S(1)} %copy-done.16, bf16[2,1536,256]{2,1,0:T(8,128)(2,1)S(1)} %bitcast.38, bf16[1536,768]{1,0:T(8,128)(2,1)S(1)} %copy-done, f32[512,768]{1,0:T(8,128)S(1)} %shard_map.63.refs_0_), custom_call_target="tpu_custom_call" | custom-call | flops 1207959552 | bytes 5242880 | tf_op jit(solution)/shard_map/pallas_call | solution.py:198
  94.5 5.5 %collective-permute-done.17 = bf16[256,768]{1,0:T(8,128)(2,1)S(1)} collective-permute-done((bf16[256,768]{1,0:T(8,128)(2,1)S(1)}, bf16[256,768]{1,0:T(8,128)(2,1)S(1)}, u32[]{:S(2)}, u32[]{:S(2)}) %collective-permute-start.17) | collective-permute-done | bytes 393248 | tf_op jit(solution)/shard_map/ppermute | solution.py:23
  100.0 2.1 %fusion.6 = (bf16[512,768]{1,0:T(8,128)(2,1)S(1)}, bf16[512,768]{1,0:T(8,128)(2,1)}) fusion(bf16[512,768]{1,0:T(8,128)(2,1)S(1)} %copy-done.18, f32[512,768]{1,0:T(8,128)S(1)} %shard_map.64, bf16[256,768]{1,0:T(8,128)(2,1)S(1)} %collective-permute-done.17, bf16[256,768]{1,0:T(8,128)(2,1)S(1)} %collective-permute-done.15), kind=kLoop, calls=%fused_computation.10 | loop fusion | flops 10616832 | bytes 4718592 | tf_op jit(solution)/shard_map/convert_element_type | solution.py:280
  102.1 2.0 %shard_map.66 = bf16[4,768,256]{2,1,0:T(8,128)(2,1)S(1)} custom-call(s32[5]{0:T(128)S(1)} %copy-done.16, bf16[512,768]{1,0:T(8,128)(2,1)S(1)} %get-tuple-element.76.g, bf16[1536,768]{1,0:T(8,128)(2,1)S(1)} %copy-done), custom_call_target="tpu_custom_call" | custom-call | flops 1207959552 | bytes 5242880 | tf_op jit(solution)/shard_map/pallas_call | solution.py:226
  104.2 1.8 collective-permute-start.19
  106.1 2.1 %shard_map.65 = bf16[4,768,256]{2,1,0:T(8,128)(2,1)S(1)} custom-call(s32[5]{0:T(128)S(1)} %copy-done.16, bf16[512,768]{1,0:T(8,128)(2,1)S(1)} %get-tuple-element.76.g, bf16[1536,768]{1,0:T(8,128)(2,1)S(1)} %copy-done.1), custom_call_target="tpu_custom_call" | custom-call | flops 1207959552 | bytes 5242880 | tf_op jit(solution)/shard_map/pallas_call | solution.py:226
  108.7 1.3 collective-permute-start.21
  110.5 3.0 %collective-permute-start.22 = (bf16[768,256]{1,0:T(8,128)(2,1)S(1)}, bf16[768,256]{1,0:T(8,128)(2,1)}, u32[]{:S(2)}, u32[]{:S(2)}) collective-permute-start(bf16[768,256]{1,0:T(8,128)(2,1)S(1)} %get-tuple-element.81), channel_id=1, source_target_pairs={{0,16},{8,24},{16,0},{24,8},{1,17},{9,25},{17,1},{25,9},{2,18},{10... | collective-permute-start | bytes 1179656 | tf_op jit(solution)/shard_map/ppermute | solution.py:23
  113.5 3.3 %shard_map.67.refs_0_ = bf16[3072,768]{1,0:T(8,128)(2,1)S(1)} custom-call(s32[5]{0:T(128)S(1)} %copy-done.16, bf16[512,768]{1,0:T(8,128)(2,1)S(1)} %get-tuple-element.76.g, bf16[2,1536,256]{2,1,0:T(8,128)(2,1)S(1)} %bitcast.35, bf16[2,1536,256]{2,1,0:T(8,128)(2,1)S(1)} %bitcast.39), custom_call_target="tpu_custom_call" | custom-call | flops 2415919104 | bytes 16777216 | tf_op jit(solution)/shard_map/pallas_call | solution.py:261
  116.8 7.4 %collective-permute-done.19.g = bf16[512,768]{1,0:T(8,128)(2,1)S(1)} collective-permute-done((bf16[512,768]{1,0:T(8,128)(2,1)S(1)}, bf16[512,768]{1,0:T(8,128)(2,1)S(1)}, u32[]{:S(2)}, u32[]{:S(2)}) %collective-permute-start.19) | collective-permute-done | bytes 786464 | tf_op jit(solution)/shard_map/ppermute | solution.py:23
  124.9 3.4 %shard_map.68 = bf16[3072,768]{1,0:T(8,128)(2,1)S(1)} custom-call(s32[5]{0:T(128)S(1)} %copy-done.16, bf16[512,768]{1,0:T(8,128)(2,1)S(1)} %collective-permute-done.19.g, bf16[2,1536,256]{2,1,0:T(8,128)(2,1)S(1)} %bitcast.37, bf16[2,1536,256]{2,1,0:T(8,128)(2,1)S(1)} %bitcast.41, bf16[3072,768]{1,0:T(8,128)(2,1)S(1)} %shard_map.67.refs_0_), custom_call_target="tpu_custom_call" | custom-call | flops 2415919104 | bytes 16777216 | tf_op jit(solution)/shard_map/pallas_call | solution.py:261
  128.3 2.2 %copy-done.3 = bf16[3072,768]{1,0:T(8,128)(2,1)} copy-done((bf16[3072,768]{1,0:T(8,128)(2,1)}, bf16[3072,768]{1,0:T(8,128)(2,1)S(1)}, u32[]{:S(2)}) %copy-start.3) | copy-done | bytes 4718616
  130.9 2.0 %shard_map.70 = bf16[4,768,256]{2,1,0:T(8,128)(2,1)S(1)} custom-call(s32[5]{0:T(128)S(1)} %copy-done.16, bf16[512,768]{1,0:T(8,128)(2,1)S(1)} %collective-permute-done.19.g, bf16[1536,768]{1,0:T(8,128)(2,1)S(1)} %copy-done), custom_call_target="tpu_custom_call" | custom-call | flops 1207959552 | bytes 5242880 | tf_op jit(solution)/shard_map/pallas_call | solution.py:226
  133.1 2.0 %shard_map.69 = bf16[4,768,256]{2,1,0:T(8,128)(2,1)S(1)} custom-call(s32[5]{0:T(128)S(1)} %copy-done.16, bf16[512,768]{1,0:T(8,128)(2,1)S(1)} %collective-permute-done.19.g, bf16[1536,768]{1,0:T(8,128)(2,1)S(1)} %copy-done.2), custom_call_target="tpu_custom_call" | custom-call | flops 1207959552 | bytes 5242880 | tf_op jit(solution)/shard_map/pallas_call | solution.py:226
  135.1 1.4 fusion.12
  137.0 1.3 collective-permute-start.26
  139.1 2.1 %collective-permute-start.24 = (bf16[768,256]{1,0:T(8,128)(2,1)S(1)}, bf16[768,256]{1,0:T(8,128)(2,1)S(1)}, u32[]{:S(2)}, u32[]{:S(2)}) collective-permute-start(bf16[768,256]{1,0:T(8,128)(2,1)S(1)} %get-tuple-element.80), channel_id=1, source_target_pairs={{0,8},{8,0},{16,24},{24,16},{1,9},{9,1},{17,25},{25,17},{2,10},{10... | collective-permute-start | bytes 1179656 | tf_op jit(solution)/shard_map/ppermute | solution.py:23
  141.2 1.7 collective-permute-start.29
  143.0 3.4 %collective-permute-start.28 = (bf16[192,256]{1,0:T(8,128)(2,1)S(1)}, bf16[192,256]{1,0:T(8,128)(2,1)S(1)}, u32[]{:S(2)}, u32[]{:S(2)}) collective-permute-start(bf16[192,256]{1,0:T(8,128)(2,1)S(1)} %get-tuple-element.88), channel_id=1, source_target_pairs={{0,4},{2,6},{4,0},{6,2},{1,5},{3,7},{5,1},{7,3},{8,12},{10,14},{12... | collective-permute-start | bytes 294920 | tf_op jit(solution)/shard_map/ppermute | solution.py:23
  146.4 4.0 %collective-permute-done.29 = bf16[192,256]{1,0:T(8,128)(2,1)S(1)} collective-permute-done((bf16[192,256]{1,0:T(8,128)(2,1)S(1)}, bf16[192,256]{1,0:T(8,128)(2,1)S(1)}, u32[]{:S(2)}, u32[]{:S(2)}) %collective-permute-start.29) | collective-permute-done | bytes 98336 | tf_op jit(solution)/shard_map/ppermute | solution.py:23
  150.4 4.7 %collective-permute-start.27 = (bf16[192,256]{1,0:T(8,128)(2,1)S(1)}, bf16[192,256]{1,0:T(8,128)(2,1)S(1)}, u32[]{:S(2)}, u32[]{:S(2)}) collective-permute-start(bf16[192,256]{1,0:T(8,128)(2,1)S(1)} %get-tuple-element.89), channel_id=1, source_target_pairs={{0,2},{2,0},{4,6},{6,4},{1,3},{3,1},{5,7},{7,5},{8,10},{10,8},{12,... | collective-permute-start | bytes 294920 | tf_op jit(solution)/shard_map/ppermute | solution.py:23
  155.1 3.7 %collective-permute-done.27 = bf16[192,256]{1,0:T(8,128)(2,1)S(1)} collective-permute-done((bf16[192,256]{1,0:T(8,128)(2,1)S(1)}, bf16[192,256]{1,0:T(8,128)(2,1)S(1)}, u32[]{:S(2)}, u32[]{:S(2)}) %collective-permute-start.27) | collective-permute-done | bytes 98336 | tf_op jit(solution)/shard_map/ppermute | solution.py:23
  159.1 3.4 %collective-permute-start.30 = (bf16[192,256]{1,0:T(8,128)(2,1)S(1)}, bf16[192,256]{1,0:T(8,128)(2,1)S(1)}, u32[]{:S(2)}, u32[]{:S(2)}) collective-permute-start(bf16[192,256]{1,0:T(8,128)(2,1)S(1)} %get-tuple-element.84), channel_id=1, source_target_pairs={{0,2},{2,0},{4,6},{6,4},{1,3},{3,1},{5,7},{7,5},{8,10},{10,8},{12,... | collective-permute-start | bytes 294920 | tf_op jit(solution)/shard_map/ppermute | solution.py:23
  162.6 3.0 %collective-permute-start.32 = (bf16[192,256]{1,0:T(8,128)(2,1)S(1)}, bf16[192,256]{1,0:T(8,128)(2,1)S(1)}, u32[]{:S(2)}, u32[]{:S(2)}) collective-permute-start(bf16[192,256]{1,0:T(8,128)(2,1)S(1)} %get-tuple-element.85), channel_id=1, source_target_pairs={{0,6},{2,4},{4,2},{6,0},{1,7},{3,5},{5,3},{7,1},{8,14},{10,12},{12... | collective-permute-start | bytes 294920 | tf_op jit(solution)/shard_map/ppermute | solution.py:23
  166.2 3.1 %collective-permute-done.32 = bf16[192,256]{1,0:T(8,128)(2,1)S(1)} collective-permute-done((bf16[192,256]{1,0:T(8,128)(2,1)S(1)}, bf16[192,256]{1,0:T(8,128)(2,1)S(1)}, u32[]{:S(2)}, u32[]{:S(2)}) %collective-permute-start.32) | collective-permute-done | bytes 98336 | tf_op jit(solution)/shard_map/ppermute | solution.py:23
  169.4 5.6 %collective-permute-done.31 = bf16[192,256]{1,0:T(8,128)(2,1)S(1)} collective-permute-done((bf16[192,256]{1,0:T(8,128)(2,1)S(1)}, bf16[192,256]{1,0:T(8,128)(2,1)S(1)}, u32[]{:S(2)}, u32[]{:S(2)}) %collective-permute-start.31) | collective-permute-done | bytes 98336 | tf_op jit(solution)/shard_map/ppermute | solution.py:23
  175.2 5.0 %collective-permute-start.33 = (bf16[192,256]{1,0:T(8,128)(2,1)S(1)}, bf16[192,256]{1,0:T(8,128)(2,1)S(1)}, u32[]{:S(2)}, u32[]{:S(2)}) collective-permute-start(bf16[192,256]{1,0:T(8,128)(2,1)S(1)} %get-tuple-element.73), channel_id=1, source_target_pairs={{0,0},{8,8},{136,16},{128,24},{24,128},{16,136},{144,144},{152,152... | collective-permute-start | bytes 294920 | tf_op jit(solution)/shard_map/ppermute | solution.py:62
  180.2 3.6 %collective-permute-done.33 = bf16[192,256]{1,0:T(8,128)(2,1)S(1)} collective-permute-done((bf16[192,256]{1,0:T(8,128)(2,1)S(1)}, bf16[192,256]{1,0:T(8,128)(2,1)S(1)}, u32[]{:S(2)}, u32[]{:S(2)}) %collective-permute-start.33) | collective-permute-done | bytes 98336 | tf_op jit(solution)/shard_map/ppermute | solution.py:62
  (101 shorter events, 21.6 us)
Async XLA Ops:
  7.2 58.9 %all-gather.2.cloned.1.call-start = ((), (), s32[]{:S(2)}) async-start(), calls=%async_computation.1 | async-start | bytes 5898240 | tf_op jit(solution)/shard_map/all_gather | solution.py:305
  7.9 176.7 %reduce-scatter.2.cloned.1.call-start = ((), (), s32[]{:S(2)}) async-start(), calls=%async_computation.2 | async-start | bytes 5898240 | tf_op jit(solution)/shard_map/reduce_scatter | solution.py:342
  8.9 9.7 %collective-permute-start.1 = (bf16[192,256]{1,0:T(8,128)(2,1)S(1)}, bf16[192,256]{1,0:T(8,128)(2,1)S(1)}, u32[]{:S(2)}, u32[]{:S(2)}) collective-permute-start(bf16[192,256]{1,0:T(8,128)(2,1)S(1)} %get-tuple-element.94), channel_id=1, source_target_pairs={{0,0},{8,8},{16,136},{24,128},{128,24},{136,16},{144,144},{152,152... | collective-permute-start | bytes 294920 | tf_op jit(solution)/shard_map/ppermute | solution.py:58
  13.4 6.4 %collective-permute-start = (bf16[192,256]{1,0:T(8,128)(2,1)S(1)}, bf16[192,256]{1,0:T(8,128)(2,1)S(1)}, u32[]{:S(2)}, u32[]{:S(2)}) collective-permute-start(bf16[192,256]{1,0:T(8,128)(2,1)S(1)} %get-tuple-element.95), channel_id=1, source_target_pairs={{0,24},{8,16},{16,144},{24,152},{128,0},{136,8},{144,136},{152,128... | collective-permute-start | bytes 294920 | tf_op jit(solution)/shard_map/ppermute | solution.py:58
  19.8 36.0 %copy-start.8 = (bf16[192,256]{1,0:T(8,128)(2,1)}, bf16[192,256]{1,0:T(8,128)(2,1)S(1)}, u32[]{:S(2)}) copy-start(bf16[192,256]{1,0:T(8,128)(2,1)S(1)} %get-tuple-element.43.refs_0_) | copy-start | bytes 294916
  19.9 10.8 %collective-permute-start.4 = (bf16[192,256]{1,0:T(8,128)(2,1)S(1)}, bf16[192,256]{1,0:T(8,128)(2,1)S(1)}, u32[]{:S(2)}, u32[]{:S(2)}) collective-permute-start(bf16[192,256]{1,0:T(8,128)(2,1)S(1)} %get-tuple-element.38.refs_0_), channel_id=1, source_target_pairs={{0,6},{2,4},{4,2},{6,0},{1,7},{3,5},{5,3},{7,1},{8,14},{10,12},{12... | collective-permute-start | bytes 294920 | tf_op jit(solution)/shard_map/ppermute | solution.py:23
  25.8 10.9 %collective-permute-start.3 = (bf16[192,256]{1,0:T(8,128)(2,1)S(1)}, bf16[192,256]{1,0:T(8,128)(2,1)S(1)}, u32[]{:S(2)}, u32[]{:S(2)}) collective-permute-start(bf16[192,256]{1,0:T(8,128)(2,1)S(1)} %get-tuple-element.38.refs_0_), channel_id=1, source_target_pairs={{0,4},{2,6},{4,0},{6,2},{1,5},{3,7},{5,1},{7,3},{8,12},{10,14},{12... | collective-permute-start | bytes 294920 | tf_op jit(solution)/shard_map/ppermute | solution.py:23
  26.8 9.9 %collective-permute-start.2 = (bf16[192,256]{1,0:T(8,128)(2,1)S(1)}, bf16[192,256]{1,0:T(8,128)(2,1)S(1)}, u32[]{:S(2)}, u32[]{:S(2)}) collective-permute-start(bf16[192,256]{1,0:T(8,128)(2,1)S(1)} %get-tuple-element.38.refs_0_), channel_id=1, source_target_pairs={{0,2},{2,0},{4,6},{6,4},{1,3},{3,1},{5,7},{7,5},{8,10},{10,8},{12,... | collective-permute-start | bytes 294920 | tf_op jit(solution)/shard_map/ppermute | solution.py:23
  37.3 17.2 %collective-permute-start.7 = (bf16[768,256]{1,0:T(8,128)(2,1)S(1)}, bf16[768,256]{1,0:T(8,128)(2,1)S(1)}, u32[]{:S(2)}, u32[]{:S(2)}) collective-permute-start(bf16[768,256]{1,0:T(8,128)(2,1)S(1)} %shard_map.58.refs_0_), channel_id=1, source_target_pairs={{0,24},{8,16},{16,8},{24,0},{1,25},{9,17},{17,9},{25,1},{2,26},{10... | collective-permute-start | bytes 1179656 | tf_op jit(solution)/shard_map/ppermute | solution.py:23
  37.4 17.1 %collective-permute-start.6 = (bf16[768,256]{1,0:T(8,128)(2,1)S(1)}, bf16[768,256]{1,0:T(8,128)(2,1)S(1)}, u32[]{:S(2)}, u32[]{:S(2)}) collective-permute-start(bf16[768,256]{1,0:T(8,128)(2,1)S(1)} %shard_map.58.refs_0_), channel_id=1, source_target_pairs={{0,16},{8,24},{16,0},{24,8},{1,17},{9,25},{17,1},{25,9},{2,18},{10... | collective-permute-start | bytes 1179656 | tf_op jit(solution)/shard_map/ppermute | solution.py:23
  38.5 16.6 %collective-permute-start.5 = (bf16[768,256]{1,0:T(8,128)(2,1)S(1)}, bf16[768,256]{1,0:T(8,128)(2,1)S(1)}, u32[]{:S(2)}, u32[]{:S(2)}) collective-permute-start(bf16[768,256]{1,0:T(8,128)(2,1)S(1)} %shard_map.58.refs_0_), channel_id=1, source_target_pairs={{0,8},{8,0},{16,24},{24,16},{1,9},{9,1},{17,25},{25,17},{2,10},{10... | collective-permute-start | bytes 1179656 | tf_op jit(solution)/shard_map/ppermute | solution.py:23
  41.4 6.8 %collective-permute-start.10 = (bf16[192,256]{1,0:T(8,128)(2,1)S(1)}, bf16[192,256]{1,0:T(8,128)(2,1)S(1)}, u32[]{:S(2)}, u32[]{:S(2)}) collective-permute-start(bf16[192,256]{1,0:T(8,128)(2,1)S(1)} %get-tuple-element.43.refs_0_), channel_id=1, source_target_pairs={{0,6},{2,4},{4,2},{6,0},{1,7},{3,5},{5,3},{7,1},{8,14},{10,12},{12... | collective-permute-start | bytes 294920 | tf_op jit(solution)/shard_map/ppermute | solution.py:23
  44.5 9.6 %collective-permute-start.9 = (bf16[192,256]{1,0:T(8,128)(2,1)S(1)}, bf16[192,256]{1,0:T(8,128)(2,1)S(1)}, u32[]{:S(2)}, u32[]{:S(2)}) collective-permute-start(bf16[192,256]{1,0:T(8,128)(2,1)S(1)} %get-tuple-element.43.refs_0_), channel_id=1, source_target_pairs={{0,4},{2,6},{4,0},{6,2},{1,5},{3,7},{5,1},{7,3},{8,12},{10,14},{12... | collective-permute-start | bytes 294920 | tf_op jit(solution)/shard_map/ppermute | solution.py:23
  48.2 7.6 %copy-start.10 = (bf16[192,256]{1,0:T(8,128)(2,1)}, bf16[192,256]{1,0:T(8,128)(2,1)S(1)}, u32[]{:S(2)}) copy-start(bf16[192,256]{1,0:T(8,128)(2,1)S(1)} %collective-permute-done.10.refs_3_) | copy-start | bytes 294916
  48.2 6.2 %collective-permute-start.8 = (bf16[192,256]{1,0:T(8,128)(2,1)S(1)}, bf16[192,256]{1,0:T(8,128)(2,1)S(1)}, u32[]{:S(2)}, u32[]{:S(2)}) collective-permute-start(bf16[192,256]{1,0:T(8,128)(2,1)S(1)} %get-tuple-element.43.refs_0_), channel_id=1, source_target_pairs={{0,2},{2,0},{4,6},{6,4},{1,3},{3,1},{5,7},{7,5},{8,10},{10,8},{12,... | collective-permute-start | bytes 294920 | tf_op jit(solution)/shard_map/ppermute | solution.py:23
  55.9 10.2 %copy-start.4 = (bf16[3072,256]{1,0:T(8,128)(2,1)}, bf16[3072,256]{1,0:T(8,128)(2,1)S(1)}, u32[]{:S(2)}) copy-start(bf16[3072,256]{1,0:T(8,128)(2,1)S(1)} %shard_map.60) | copy-start | bytes 4718596
  55.9 9.2 %collective-permute-start.14 = (bf16[3072,256]{1,0:T(8,128)(2,1)S(1)}, bf16[3072,256]{1,0:T(8,128)(2,1)S(1)}, u32[]{:S(2)}, u32[]{:S(2)}) collective-permute-start(bf16[3072,256]{1,0:T(8,128)(2,1)S(1)} %shard_map.60), channel_id=1, source_target_pairs={{0,1},{1,0},{2,3},{3,2},{4,5},{5,4},{6,7},{7,6},{8,9},{9,8},{10,11... | collective-permute-start | bytes 4718600 | tf_op jit(solution)/shard_map/ppermute | solution.py:23
  60.9 21.2 %collective-permute-start.13 = (bf16[768,256]{1,0:T(8,128)(2,1)S(1)}, bf16[768,256]{1,0:T(8,128)(2,1)}, u32[]{:S(2)}, u32[]{:S(2)}) collective-permute-start(bf16[768,256]{1,0:T(8,128)(2,1)S(1)} %shard_map.59.refs_0_), channel_id=1, source_target_pairs={{0,24},{8,16},{16,8},{24,0},{1,25},{9,17},{17,9},{25,1},{2,26},{10... | collective-permute-start | bytes 1179656 | tf_op jit(solution)/shard_map/ppermute | solution.py:23
  63.6 18.5 %collective-permute-start.12 = (bf16[768,256]{1,0:T(8,128)(2,1)S(1)}, bf16[768,256]{1,0:T(8,128)(2,1)}, u32[]{:S(2)}, u32[]{:S(2)}) collective-permute-start(bf16[768,256]{1,0:T(8,128)(2,1)S(1)} %shard_map.59.refs_0_), channel_id=1, source_target_pairs={{0,16},{8,24},{16,0},{24,8},{1,17},{9,25},{17,1},{25,9},{2,18},{10... | collective-permute-start | bytes 1179656 | tf_op jit(solution)/shard_map/ppermute | solution.py:23
  64.2 18.5 %collective-permute-start.11 = (bf16[768,256]{1,0:T(8,128)(2,1)S(1)}, bf16[768,256]{1,0:T(8,128)(2,1)}, u32[]{:S(2)}, u32[]{:S(2)}) collective-permute-start(bf16[768,256]{1,0:T(8,128)(2,1)S(1)} %shard_map.59.refs_0_), channel_id=1, source_target_pairs={{0,8},{8,0},{16,24},{24,16},{1,9},{9,1},{17,25},{25,17},{2,10},{10... | collective-permute-start | bytes 1179656 | tf_op jit(solution)/shard_map/ppermute | solution.py:23
  74.3 14.1 %copy-start.21 = (bf16[256,768]{1,0:T(8,128)(2,1)S(1)}, bf16[256,768]{1,0:T(8,128)(2,1)}, u32[]{:S(2)}) copy-start(bf16[256,768]{1,0:T(8,128)(2,1)} %get-tuple-element.59) | copy-start | bytes 1179652
  74.3 16.1 %copy-start.1 = (bf16[1536,768]{1,0:T(8,128)(2,1)S(1)}, bf16[1536,768]{1,0:T(8,128)(2,1)}, u32[]{:S(2)}) copy-start(bf16[1536,768]{1,0:T(8,128)(2,1)} %get-tuple-element.57.w) | copy-start | bytes 7077892
  74.3 16.1 %copy-start.16 = (s32[5]{0:T(128)S(1)}, s32[5]{0:T(128)}, u32[]{:S(2)}) copy-start(s32[5]{0:T(128)} %stack.23.idx) | copy-start | bytes 64
  74.3 12.5 %collective-permute-start.15 = (bf16[256,768]{1,0:T(8,128)(2,1)}, bf16[256,768]{1,0:T(8,128)(2,1)S(1)}, u32[]{:S(2)}, u32[]{:S(2)}) collective-permute-start(bf16[256,768]{1,0:T(8,128)(2,1)} %get-tuple-element.51), channel_id=1, source_target_pairs={{0,128},{128,0},{1,129},{129,1},{2,130},{130,2},{3,131},{131,3},{4... | collective-permute-start | bytes 1179656 | tf_op jit(solution)/shard_map/ppermute | solution.py:23
  88.3 4.1 %collective-permute-start.16 = (bf16[3072,256]{1,0:T(8,128)(2,1)S(1)}, bf16[3072,256]{1,0:T(8,128)(2,1)S(1)}, u32[]{:S(2)}, u32[]{:S(2)}) collective-permute-start(bf16[3072,256]{1,0:T(8,128)(2,1)S(1)} %shard_map.62), channel_id=1, source_target_pairs={{0,1},{1,0},{2,3},{3,2},{4,5},{5,4},{6,7},{7,6},{8,9},{9,8},{10,11... | collective-permute-start | bytes 4718600 | tf_op jit(solution)/shard_map/ppermute | solution.py:23
  88.4 11.5 %collective-permute-start.17 = (bf16[256,768]{1,0:T(8,128)(2,1)S(1)}, bf16[256,768]{1,0:T(8,128)(2,1)S(1)}, u32[]{:S(2)}, u32[]{:S(2)}) collective-permute-start(bf16[256,768]{1,0:T(8,128)(2,1)S(1)} %copy-done.21), channel_id=1, source_target_pairs={{0,128},{128,0},{1,129},{129,1},{2,130},{130,2},{3,131},{131,3},{4... | collective-permute-start | bytes 1179656 | tf_op jit(solution)/shard_map/ppermute | solution.py:23
  92.5 7.5 %copy-start.18 = (bf16[512,768]{1,0:T(8,128)(2,1)S(1)}, bf16[512,768]{1,0:T(8,128)(2,1)}, u32[]{:S(2)}) copy-start(bf16[512,768]{1,0:T(8,128)(2,1)} %param.5) | copy-start | bytes 2359300
  104.1 4.0 %collective-permute-start.18 = (bf16[4,768,256]{2,1,0:T(8,128)(2,1)S(1)}, bf16[4,768,256]{2,1,0:T(8,128)(2,1)S(1)}, u32[]{:S(2)}, u32[]{:S(2)}) collective-permute-start(bf16[4,768,256]{2,1,0:T(8,128)(2,1)S(1)} %shard_map.66), channel_id=1, source_target_pairs={{0,1},{1,0},{2,3},{3,2},{4,5},{5,4},{6,7},{7,6},{8,9},{9,8},{10,11... | collective-permute-start | bytes 4718600 | tf_op jit(solution)/shard_map/ppermute | solution.py:23
  104.2 20.0 %collective-permute-start.19 = (bf16[512,768]{1,0:T(8,128)(2,1)S(1)}, bf16[512,768]{1,0:T(8,128)(2,1)S(1)}, u32[]{:S(2)}, u32[]{:S(2)}) collective-permute-start(bf16[512,768]{1,0:T(8,128)(2,1)S(1)} %get-tuple-element.76.g), channel_id=1, source_target_pairs={{0,128},{128,0},{1,129},{129,1},{2,130},{130,2},{3,131},{131,3},{4... | collective-permute-start | bytes 2359304 | tf_op jit(solution)/shard_map/ppermute | solution.py:23
  108.7 15.5 %collective-permute-start.21 = (bf16[768,256]{1,0:T(8,128)(2,1)S(1)}, bf16[768,256]{1,0:T(8,128)(2,1)S(1)}, u32[]{:S(2)}, u32[]{:S(2)}) collective-permute-start(bf16[768,256]{1,0:T(8,128)(2,1)S(1)} %get-tuple-element.82), channel_id=1, source_target_pairs={{0,24},{8,16},{16,8},{24,0},{1,25},{9,17},{17,9},{25,1},{2,26},{10... | collective-permute-start | bytes 1179656 | tf_op jit(solution)/shard_map/ppermute | solution.py:23
  110.0 15.0 %collective-permute-start.20 = (bf16[768,256]{1,0:T(8,128)(2,1)S(1)}, bf16[768,256]{1,0:T(8,128)(2,1)}, u32[]{:S(2)}, u32[]{:S(2)}) collective-permute-start(bf16[768,256]{1,0:T(8,128)(2,1)S(1)} %get-tuple-element.83), channel_id=1, source_target_pairs={{0,8},{8,0},{16,24},{24,16},{1,9},{9,1},{17,25},{25,17},{2,10},{10... | collective-permute-start | bytes 1179656 | tf_op jit(solution)/shard_map/ppermute | solution.py:23
  110.5 14.4 %copy-start.5 = (bf16[3072,256]{1,0:T(8,128)(2,1)S(1)}, bf16[3072,256]{1,0:T(8,128)(2,1)}, u32[]{:S(2)}) copy-start(bf16[3072,256]{1,0:T(8,128)(2,1)} %copy-done.4) | copy-start | bytes 4718596
  110.5 14.4 %copy-start.7 = (bf16[3072,256]{1,0:T(8,128)(2,1)S(1)}, bf16[3072,256]{1,0:T(8,128)(2,1)}, u32[]{:S(2)}) copy-start(bf16[3072,256]{1,0:T(8,128)(2,1)} %copy-done.6) | copy-start | bytes 4718596
  110.5 20.3 %collective-permute-start.22 = (bf16[768,256]{1,0:T(8,128)(2,1)S(1)}, bf16[768,256]{1,0:T(8,128)(2,1)}, u32[]{:S(2)}, u32[]{:S(2)}) collective-permute-start(bf16[768,256]{1,0:T(8,128)(2,1)S(1)} %get-tuple-element.81), channel_id=1, source_target_pairs={{0,16},{8,24},{16,0},{24,8},{1,17},{9,25},{17,1},{25,9},{2,18},{10... | collective-permute-start | bytes 1179656 | tf_op jit(solution)/shard_map/ppermute | solution.py:23
  128.3 2.2 %copy-start.3 = (bf16[3072,768]{1,0:T(8,128)(2,1)}, bf16[3072,768]{1,0:T(8,128)(2,1)S(1)}, u32[]{:S(2)}) copy-start(bf16[3072,768]{1,0:T(8,128)(2,1)S(1)} %shard_map.68) | copy-start | bytes 14155780
  130.9 2.2 %copy-start.2 = (bf16[1536,768]{1,0:T(8,128)(2,1)S(1)}, bf16[1536,768]{1,0:T(8,128)(2,1)}, u32[]{:S(2)}) copy-start(bf16[1536,768]{1,0:T(8,128)(2,1)} %get-tuple-element.57.w) | copy-start | bytes 7077892
  132.9 3.6 %collective-permute-start.23 = (bf16[4,768,256]{2,1,0:T(8,128)(2,1)S(1)}, bf16[4,768,256]{2,1,0:T(8,128)(2,1)S(1)}, u32[]{:S(2)}, u32[]{:S(2)}) collective-permute-start(bf16[4,768,256]{2,1,0:T(8,128)(2,1)S(1)} %shard_map.70), channel_id=1, source_target_pairs={{0,1},{1,0},{2,3},{3,2},{4,5},{5,4},{6,7},{7,6},{8,9},{9,8},{10,11... | collective-permute-start | bytes 4718600 | tf_op jit(solution)/shard_map/ppermute | solution.py:23
  137.0 21.8 %collective-permute-start.26 = (bf16[768,256]{1,0:T(8,128)(2,1)S(1)}, bf16[768,256]{1,0:T(8,128)(2,1)S(1)}, u32[]{:S(2)}, u32[]{:S(2)}) collective-permute-start(bf16[768,256]{1,0:T(8,128)(2,1)S(1)} %get-tuple-element.78), channel_id=1, source_target_pairs={{0,24},{8,16},{16,8},{24,0},{1,25},{9,17},{17,9},{25,1},{2,26},{10... | collective-permute-start | bytes 1179656 | tf_op jit(solution)/shard_map/ppermute | solution.py:23
  138.3 20.5 %collective-permute-start.25 = (bf16[768,256]{1,0:T(8,128)(2,1)S(1)}, bf16[768,256]{1,0:T(8,128)(2,1)S(1)}, u32[]{:S(2)}, u32[]{:S(2)}) collective-permute-start(bf16[768,256]{1,0:T(8,128)(2,1)S(1)} %get-tuple-element.79), channel_id=1, source_target_pairs={{0,16},{8,24},{16,0},{24,8},{1,17},{9,25},{17,1},{25,9},{2,18},{10... | collective-permute-start | bytes 1179656 | tf_op jit(solution)/shard_map/ppermute | solution.py:23
  139.1 19.8 %collective-permute-start.24 = (bf16[768,256]{1,0:T(8,128)(2,1)S(1)}, bf16[768,256]{1,0:T(8,128)(2,1)S(1)}, u32[]{:S(2)}, u32[]{:S(2)}) collective-permute-start(bf16[768,256]{1,0:T(8,128)(2,1)S(1)} %get-tuple-element.80), channel_id=1, source_target_pairs={{0,8},{8,0},{16,24},{24,16},{1,9},{9,1},{17,25},{25,17},{2,10},{10... | collective-permute-start | bytes 1179656 | tf_op jit(solution)/shard_map/ppermute | solution.py:23
  141.2 9.2 %collective-permute-start.29 = (bf16[192,256]{1,0:T(8,128)(2,1)S(1)}, bf16[192,256]{1,0:T(8,128)(2,1)S(1)}, u32[]{:S(2)}, u32[]{:S(2)}) collective-permute-start(bf16[192,256]{1,0:T(8,128)(2,1)S(1)} %get-tuple-element.87), channel_id=1, source_target_pairs={{0,6},{2,4},{4,2},{6,0},{1,7},{3,5},{5,3},{7,1},{8,14},{10,12},{12... | collective-permute-start | bytes 294920 | tf_op jit(solution)/shard_map/ppermute | solution.py:23
  143.0 12.1 %collective-permute-start.28 = (bf16[192,256]{1,0:T(8,128)(2,1)S(1)}, bf16[192,256]{1,0:T(8,128)(2,1)S(1)}, u32[]{:S(2)}, u32[]{:S(2)}) collective-permute-start(bf16[192,256]{1,0:T(8,128)(2,1)S(1)} %get-tuple-element.88), channel_id=1, source_target_pairs={{0,4},{2,6},{4,0},{6,2},{1,5},{3,7},{5,1},{7,3},{8,12},{10,14},{12... | collective-permute-start | bytes 294920 | tf_op jit(solution)/shard_map/ppermute | solution.py:23
  150.4 8.4 %collective-permute-start.27 = (bf16[192,256]{1,0:T(8,128)(2,1)S(1)}, bf16[192,256]{1,0:T(8,128)(2,1)S(1)}, u32[]{:S(2)}, u32[]{:S(2)}) collective-permute-start(bf16[192,256]{1,0:T(8,128)(2,1)S(1)} %get-tuple-element.89), channel_id=1, source_target_pairs={{0,2},{2,0},{4,6},{6,4},{1,3},{3,1},{5,7},{7,5},{8,10},{10,8},{12,... | collective-permute-start | bytes 294920 | tf_op jit(solution)/shard_map/ppermute | solution.py:23
  159.1 7.1 %collective-permute-start.30 = (bf16[192,256]{1,0:T(8,128)(2,1)S(1)}, bf16[192,256]{1,0:T(8,128)(2,1)S(1)}, u32[]{:S(2)}, u32[]{:S(2)}) collective-permute-start(bf16[192,256]{1,0:T(8,128)(2,1)S(1)} %get-tuple-element.84), channel_id=1, source_target_pairs={{0,2},{2,0},{4,6},{6,4},{1,3},{3,1},{5,7},{7,5},{8,10},{10,8},{12,... | collective-permute-start | bytes 294920 | tf_op jit(solution)/shard_map/ppermute | solution.py:23
  162.6 6.8 %collective-permute-start.32 = (bf16[192,256]{1,0:T(8,128)(2,1)S(1)}, bf16[192,256]{1,0:T(8,128)(2,1)S(1)}, u32[]{:S(2)}, u32[]{:S(2)}) collective-permute-start(bf16[192,256]{1,0:T(8,128)(2,1)S(1)} %get-tuple-element.85), channel_id=1, source_target_pairs={{0,6},{2,4},{4,2},{6,0},{1,7},{3,5},{5,3},{7,1},{8,14},{10,12},{12... | collective-permute-start | bytes 294920 | tf_op jit(solution)/shard_map/ppermute | solution.py:23
  165.6 9.4 %collective-permute-start.31 = (bf16[192,256]{1,0:T(8,128)(2,1)S(1)}, bf16[192,256]{1,0:T(8,128)(2,1)S(1)}, u32[]{:S(2)}, u32[]{:S(2)}) collective-permute-start(bf16[192,256]{1,0:T(8,128)(2,1)S(1)} %get-tuple-element.86), channel_id=1, source_target_pairs={{0,4},{2,6},{4,0},{6,2},{1,5},{3,7},{5,1},{7,3},{8,12},{10,14},{12... | collective-permute-start | bytes 294920 | tf_op jit(solution)/shard_map/ppermute | solution.py:23
  175.1 5.1 %collective-permute-start.34 = (bf16[192,256]{1,0:T(8,128)(2,1)S(1)}, bf16[192,256]{1,0:T(8,128)(2,1)S(1)}, u32[]{:S(2)}, u32[]{:S(2)}) collective-permute-start(bf16[192,256]{1,0:T(8,128)(2,1)S(1)} %broadcast_select_fusion.4), channel_id=1, source_target_pairs={{24,0},{16,8},{144,16},{152,24},{0,128},{8,136},{136,144},{128,152... | collective-permute-start | bytes 294920 | tf_op jit(solution)/shard_map/ppermute | solution.py:62
  175.2 8.6 %collective-permute-start.33 = (bf16[192,256]{1,0:T(8,128)(2,1)S(1)}, bf16[192,256]{1,0:T(8,128)(2,1)S(1)}, u32[]{:S(2)}, u32[]{:S(2)}) collective-permute-start(bf16[192,256]{1,0:T(8,128)(2,1)S(1)} %get-tuple-element.73), channel_id=1, source_target_pairs={{0,0},{8,8},{136,16},{128,24},{24,128},{16,136},{144,144},{152,152... | collective-permute-start | bytes 294920 | tf_op jit(solution)/shard_map/ppermute | solution.py:62
  (11 other events, 14.9 us)
Sparse Core Ops, SparseCore 0:
  9.8 56.2 all-gather.1
  131.0 51.7 reduce-scatter.1
